TPU v7x, 32 devices: a whole 2x2x4 slice. The times are simulated.
32 devices in a mesh: gz: 16 (over z, y, x), gy: 2 (over core).
Axes of the slice: x: 2, y: 2, z: 4, core: 2. Of those that a mesh axis runs over, the one named last changes fastest.
Arguments:
- fields: float32 [4, 64, 32, 512], P(None, 'gz', 'gy'), may hold values from -4 to 4
- velocity: float32 [2, 64, 32, 512], P(None, 'gz', 'gy'), may hold values from -3 to 3
- face_rate: float32 [64, 32, 512], P('gz', 'gy'), may hold values from 1 to 4
- xy_rate: float32 [4], replicated, may hold values from 0.05 to 0.2
- z_scale: float32 [4], replicated, may hold values from 8 to 32
Outputs:
- advanced: float32 [4, 64, 32, 512], P(None, 'gz', 'gy')
All inputs are finite; a program needn't handle non-finite values.
Results may differ from a plain program's by a relative error of at most 0.0003.
Values sent between devices are 32-bit elements; how exact they have to be, the bound alone decides.
A program may use at most 64 MiB of HBM per device.

v0:
```python
import jax
import jax.numpy as jnp
from jax import lax
from jax.sharding import PartitionSpec as P

STEPS = 2


def with_halo(block, sides, width):
    for axis, dim in sides:
        count = lax.axis_size(axis)
        forward = [(i, i + 1) for i in range(count - 1)]
        forward.append((count - 1, 0))
        backward = [(target, source) for source, target in forward]
        low = lax.ppermute(
            lax.slice_in_dim(block, block.shape[dim] - width, None, axis=dim), axis, forward
        )
        high = lax.ppermute(lax.slice_in_dim(block, 0, width, axis=dim), axis, backward)
        block = jnp.concatenate([low, block, high], axis=dim)
    return block


def tendency(extended, along_x, along_y, spread):
    middle = extended[:, :, 1:-1]
    north = extended[:, :, 2:]
    south = extended[:, :, :-2]
    eastern = jnp.roll(middle, -1, 3)
    western = jnp.roll(middle, 1, 3)
    return spread * (eastern + western + north + south - 4.0 * middle) - 0.5 * (
        along_x * (eastern - western) + along_y * (north - south)
    )


def reduce_step(current, beneath, overhead):
    couple_down = current[0]
    couple_up = current[1]
    pivot = 1.0 - couple_down * beneath[1] - couple_up * overhead[0]
    return jnp.stack(
        [
            -couple_down * beneath[0] / pivot,
            -couple_up * overhead[1] / pivot,
            (current[2] - couple_down * beneath[2] - couple_up * overhead[2]) / pivot,
        ]
    )


def offset_rows(values, offset, axis):
    length = values.shape[axis]
    zeros_block = jnp.zeros_like(lax.slice_in_dim(values, 0, abs(offset), axis=axis))
    if offset > 0:
        return jnp.concatenate(
            [zeros_block, lax.slice_in_dim(values, 0, length - offset, axis=axis)], axis
        )
    return jnp.concatenate(
        [lax.slice_in_dim(values, -offset, length, axis=axis), zeros_block], axis
    )


def local_reduce(system, axis):
    length = system.shape[axis]
    distance = 1
    while distance < length:
        system = reduce_step(
            system, offset_rows(system, distance, axis), offset_rows(system, -distance, axis)
        )
        distance = distance * 2
    return system[2]


def on_device(fields, velocity, face_rate, xy_rate, z_scale):
    spread = xy_rate[:, None, None, None]
    present = fields
    for step_index in range(STEPS):
        along_x = velocity[0][None]
        along_y = velocity[1][None]
        extended = with_halo(present, (("gy", 2),), 1)
        sectioned = present + tendency(extended, along_x, along_y, spread)
        extended = with_halo(sectioned, (("gy", 2),), 1)
        explicit = 0.5 * present + 0.5 * (sectioned + tendency(extended, along_x, along_y, spread))
        groups = lax.axis_size("gz")
        field_total, layers, rows_y, columns_x = explicit.shape
        block = rows_y * columns_x // groups
        shaped = explicit.reshape(field_total, layers, groups, 1, block)
        rates = face_rate.reshape(1, layers, groups, 1, block)
        values = lax.all_to_all(shaped, "gz", split_axis=2, concat_axis=3, tiled=True)
        rates_piece = lax.all_to_all(rates, "gz", split_axis=2, concat_axis=3, tiled=True)
        sources = values.shape[3]
        columns = values.shape[4]
        column_values = jnp.transpose(values[:, :, 0], (0, 2, 1, 3)).reshape(
            field_total, sources * layers, columns
        )
        column_rates = jnp.transpose(rates_piece[:, :, 0], (0, 2, 1, 3)).reshape(
            1, sources * layers, columns
        )
        below_faces = z_scale[:, None, None] * column_rates
        above_faces = jnp.concatenate([below_faces[:, 1:], jnp.zeros_like(below_faces[:, :1])], 1)
        diagonal = 1.0 + below_faces + above_faces
        system = jnp.stack(
            [-below_faces / diagonal, -above_faces / diagonal, column_values / diagonal]
        )
        solution = local_reduce(system, 2)
        solved = jnp.transpose(
            solution.reshape(field_total, sources, layers, columns), (0, 2, 1, 3)
        )[:, :, None]
        present = lax.all_to_all(solved, "gz", split_axis=3, concat_axis=2, tiled=True).reshape(
            explicit.shape
        )
    return present


def solution(mesh):
    in_specs = (P(None, "gz", "gy", None), P(None, "gz", "gy", None), P("gz", "gy", None), P(), P())
    out_specs = P(None, "gz", "gy", None)
    return jax.shard_map(
        on_device, mesh=mesh, in_specs=in_specs, out_specs=out_specs, check_vma=False
    )
```

profile of v0, /device:TPU:0, one launch (start us, length us, event | category | flops | bytes accessed | tf_op | source)
XLA Modules:
  0.0 120.9 jit_solution(12246072780128319218)
XLA Ops:
  0.0 1.6 %copy.41 = f32[4,16,512]{2,0,1:T(4,128)} copy(f32[4,16,512]{2,1,0:T(8,128)} %param.7) | data formatting | bytes 262144 | tf_op args[2]
  1.6 8.3 %all-to-all-start.1 = ((f32[1,4,16,1,512]{4,1,3,0,2:T(4,128)}), f32[1,4,16,1,512]{4,1,3,0,2:T(4,128)S(1)}, u32[]{:S(2)}, u32[]{:S(2)}) async-start(f32[1,4,16,1,512]{4,1,3,0,2:T(4,128)} %bitcast.684), calls=%async_computation.1 | async-start | bytes 262144 | tf_op jit(solution)/shard_map/all_to_all | solution.py:86
  10.0 1.4 %copy.33 = f32[4,4,16,512]{3,0,1,2:T(4,128)S(1)} copy(f32[4,4,16,512]{3,2,1,0:T(8,128)} %param.5) | data formatting | bytes 1048576 | tf_op args[0]
  11.4 0.5 collective-permute-start.1
  12.1 0.3 fusion.239
  12.8 0.8 subtract_add_fusion.1
  13.6 0.3 fusion.236
  14.0 0.4 collective-permute-start.2
  14.7 0.6 collective-permute-done.2
  15.2 0.3 collective-permute-done.3
  15.6 1.8 %multiply_bitcast_fusion.1 = f32[4,4,16,1,512]{4,0,1,3,2:T(4,128)} fusion(f32[4,4,16,512]{3,0,1,2:T(4,128)S(1)} %subtract_add_fusion.1, f32[4,4,1,512]{3,0,1,2:T(4,128)S(1)} %collective-permute-done.3, f32[4,4,1,512]{3,0,1,2:T(4,128)S(1)} %collective-permute-done.2, f32[4,4,16,511]{3,0,1,2:T(4,128)S(1)} %get-tuple-element.75, ...), kind=kLoop, calls=%fused_computation.320 | loop fusion | flops 2621440 | bytes 2949136 | tf_op jit(solution)/shard_map/reshape | solution.py:83
  17.4 0.4 all-to-all-done.1
  17.8 6.5 %all-to-all-start = ((f32[4,4,16,1,512]{4,0,1,3,2:T(4,128)}), f32[4,4,16,1,512]{4,0,1,3,2:T(4,128)S(1)}, u32[]{:S(2)}, u32[]{:S(2)}) async-start(f32[4,4,16,1,512]{4,0,1,3,2:T(4,128)} %multiply_bitcast_fusion.1), calls=%async_computation | async-start | bytes 1048576 | tf_op jit(solution)/shard_map/all_to_all | solution.py:85
  24.5 15.2 %all-to-all-done = f32[4,4,16,1,512]{4,0,1,3,2:T(4,128)S(1)} async-done(((f32[4,4,16,1,512]{4,0,1,3,2:T(4,128)}), f32[4,4,16,1,512]{4,0,1,3,2:T(4,128)S(1)}, u32[]{:S(2)}, u32[]{:S(2)}) %all-to-all-start) | async-done | bytes 524320 | tf_op jit(solution)/shard_map/all_to_all | solution.py:85
  39.7 0.5 fusion.217
  40.2 0.4 pad_maximum_fusion
  40.5 0.5 fusion.229
  41.1 1.0 fusion.18
  42.1 0.4 pad_maximum_fusion.2
  42.4 0.6 fusion.228
  43.0 0.7 fusion.56
  43.8 0.4 pad_maximum_fusion.3
  44.1 0.5 fusion.227
  44.6 0.7 fusion.94
  45.4 0.4 pad_maximum_fusion.4
  45.7 0.5 fusion.226
  46.2 0.7 fusion.132
  46.9 0.4 pad_maximum_fusion.5
  47.3 0.4 fusion.225
  47.7 0.7 fusion.170
  48.4 0.4 pad_maximum_fusion.6
  49.1 0.4 fusion.194
  49.4 18.2 %all_to_all.20 = f32[4,4,1,16,512]{4,0,1,2,3:T(4,128)S(1)} all-to-all(f32[4,4,1,16,512]{4,0,1,2,3:T(4,128)S(1)} %bitcast.721), channel_id=1, replica_groups=mesh['gz'=16,'gy'=2] {'gz'}, dimensions={3} | all-to-all | bytes 1048576 | tf_op jit(solution)/shard_map/all_to_all | solution.py:105
  67.6 0.3 fusion.233
  68.0 0.5 collective-permute-start.5
  68.6 0.6 collective-permute-done.4
  69.4 0.8 subtract_add_fusion
  70.2 0.3 fusion.230
  70.5 0.4 collective-permute-start.6
  71.2 0.6 collective-permute-done.6
  71.8 0.3 collective-permute-done.7
  72.1 0.8 multiply_bitcast_fusion
  73.0 19.1 %all_to_all.21 = f32[4,4,16,1,512]{4,0,1,3,2:T(4,128)S(1)} all-to-all(f32[4,4,16,1,512]{4,0,1,3,2:T(4,128)S(1)} %multiply_bitcast_fusion), channel_id=1, replica_groups=mesh['gz'=16,'gy'=2] {'gz'}, dimensions={2} | all-to-all | bytes 1048576 | tf_op jit(solution)/shard_map/all_to_all | solution.py:85
  92.0 0.3 bitcast_divide_fusion
  92.4 0.4 pad_maximum_fusion.7
  92.7 0.5 fusion.223
  93.3 1.0 fusion.37
  94.3 0.4 pad_maximum_fusion.8
  94.6 0.6 fusion.222
  95.2 0.7 fusion.75
  95.9 0.4 pad_maximum_fusion.9
  96.3 0.5 fusion.221
  96.8 0.7 fusion.113
  97.6 0.4 pad_maximum_fusion.10
  97.9 0.5 fusion.220
  98.4 0.7 fusion.151
  99.1 0.4 pad_maximum_fusion.11
  99.5 0.4 fusion.219
  99.9 0.7 fusion.189
  100.6 0.4 pad_maximum_fusion.12
  101.0 0.3 fusion.218
  101.3 0.4 fusion.207
  101.6 18.2 %all_to_all.22 = f32[4,4,1,16,512]{4,0,1,2,3:T(4,128)S(1)} all-to-all(f32[4,4,1,16,512]{4,0,1,2,3:T(4,128)S(1)} %bitcast.722), channel_id=1, replica_groups=mesh['gz'=16,'gy'=2] {'gz'}, dimensions={3} | all-to-all | bytes 1048576 | tf_op jit(solution)/shard_map/all_to_all | solution.py:105
  119.8 1.1 copy.38
  (30 shorter events, 2.0 us)
Async XLA Ops:
  1.6 16.1 %all-to-all-start.1 = ((f32[1,4,16,1,512]{4,1,3,0,2:T(4,128)}), f32[1,4,16,1,512]{4,1,3,0,2:T(4,128)S(1)}, u32[]{:S(2)}, u32[]{:S(2)}) async-start(f32[1,4,16,1,512]{4,1,3,0,2:T(4,128)} %bitcast.684), calls=%async_computation.1 | async-start | bytes 262144 | tf_op jit(solution)/shard_map/all_to_all | solution.py:86
  11.3 1.1 copy-start.1
  11.4 1.3 %collective-permute-start = (f32[4,4,1,512]{3,0,1,2:T(4,128)S(1)}, f32[4,4,1,512]{3,0,1,2:T(4,128)S(1)}, u32[]{:S(2)}, u32[]{:S(2)}) collective-permute-start(f32[4,4,1,512]{3,0,1,2:T(4,128)S(1)} %get-tuple-element.84), channel_id=1, source_target_pairs={{1,0},{0,1},{3,2},{2,3},{5,4},{4,5},{7,6},{6,7},{9,8},{8,9},{11,10... | collective-permute-start | bytes 98312 | tf_op jit(solution)/shard_map/ppermute | solution.py:18
  11.4 1.4 %collective-permute-start.1 = (f32[4,4,1,512]{3,0,1,2:T(4,128)S(1)}, f32[4,4,1,512]{3,0,1,2:T(4,128)S(1)}, u32[]{:S(2)}, u32[]{:S(2)}) collective-permute-start(f32[4,4,1,512]{3,0,1,2:T(4,128)S(1)} %get-tuple-element.85), channel_id=1, source_target_pairs={{0,1},{1,0},{2,3},{3,2},{4,5},{5,4},{6,7},{7,6},{8,9},{9,8},{10,11... | collective-permute-start | bytes 98312 | tf_op jit(solution)/shard_map/ppermute | solution.py:15
  12.1 0.7 copy-start.3
  13.6 2.0 %copy-start = (f32[4,4,16,512]{3,2,1,0:T(8,128)S(1)}, f32[4,4,16,512]{3,2,1,0:T(8,128)}, u32[]{:S(2)}) copy-start(f32[4,4,16,512]{3,2,1,0:T(8,128)} %param.5) | copy-start | bytes 1572868
  14.0 1.3 %collective-permute-start.2 = (f32[4,4,1,512]{3,0,1,2:T(4,128)S(1)}, f32[4,4,1,512]{3,0,1,2:T(4,128)S(1)}, u32[]{:S(2)}, u32[]{:S(2)}) collective-permute-start(f32[4,4,1,512]{3,0,1,2:T(4,128)S(1)} %get-tuple-element.78), channel_id=1, source_target_pairs={{1,0},{0,1},{3,2},{2,3},{5,4},{4,5},{7,6},{6,7},{9,8},{8,9},{11,10... | collective-permute-start | bytes 98312 | tf_op jit(solution)/shard_map/ppermute | solution.py:18
  14.4 1.2 collective-permute-start.3
  15.6 8.7 %copy-start.2 = (f32[4]{0:T(128)S(1)}, f32[4]{0:T(128)}, u32[]{:S(2)}) copy-start(f32[4]{0:T(128)} %param.9) | copy-start | bytes 52
  17.8 21.9 %all-to-all-start = ((f32[4,4,16,1,512]{4,0,1,3,2:T(4,128)}), f32[4,4,16,1,512]{4,0,1,3,2:T(4,128)S(1)}, u32[]{:S(2)}, u32[]{:S(2)}) async-start(f32[4,4,16,1,512]{4,0,1,3,2:T(4,128)} %multiply_bitcast_fusion.1), calls=%async_computation | async-start | bytes 1048576 | tf_op jit(solution)/shard_map/all_to_all | solution.py:85
  67.9 1.3 %collective-permute-start.4 = (f32[4,4,1,512]{3,0,1,2:T(4,128)S(1)}, f32[4,4,1,512]{3,0,1,2:T(4,128)S(1)}, u32[]{:S(2)}, u32[]{:S(2)}) collective-permute-start(f32[4,4,1,512]{3,0,1,2:T(4,128)S(1)} %get-tuple-element.72), channel_id=1, source_target_pairs={{1,0},{0,1},{3,2},{2,3},{5,4},{4,5},{7,6},{6,7},{9,8},{8,9},{11,10... | collective-permute-start | bytes 98312 | tf_op jit(solution)/shard_map/ppermute | solution.py:18
  68.0 1.4 %collective-permute-start.5 = (f32[4,4,1,512]{3,0,1,2:T(4,128)S(1)}, f32[4,4,1,512]{3,0,1,2:T(4,128)S(1)}, u32[]{:S(2)}, u32[]{:S(2)}) collective-permute-start(f32[4,4,1,512]{3,0,1,2:T(4,128)S(1)} %get-tuple-element.73), channel_id=1, source_target_pairs={{0,1},{1,0},{2,3},{3,2},{4,5},{5,4},{6,7},{7,6},{8,9},{9,8},{10,11... | collective-permute-start | bytes 98312 | tf_op jit(solution)/shard_map/ppermute | solution.py:15
  70.5 1.3 %collective-permute-start.6 = (f32[4,4,1,512]{3,0,1,2:T(4,128)S(1)}, f32[4,4,1,512]{3,0,1,2:T(4,128)S(1)}, u32[]{:S(2)}, u32[]{:S(2)}) collective-permute-start(f32[4,4,1,512]{3,0,1,2:T(4,128)S(1)} %get-tuple-element.66), channel_id=1, source_target_pairs={{1,0},{0,1},{3,2},{2,3},{5,4},{4,5},{7,6},{6,7},{9,8},{8,9},{11,10... | collective-permute-start | bytes 98312 | tf_op jit(solution)/shard_map/ppermute | solution.py:18
  70.9 1.2 collective-permute-start.7
where the time goes:
time: 121 us
  blocking collectives  55.4 us (46%)
  waiting for transfers between devices  18.2 us (15%)
  other arithmetic  17.8 us (15%)
  starting transfers between devices  17.1 us (14%)
  local copies, waits for them, and re-layouts  11.9 us (10%)
    all_to_all x2, blocking collectives, on_device(): lax.all_to_all(solved, 'gz', split_axis=3, concat_axis=2, tiled=True)  36.4 us
    all_to_all x1, blocking collectives, on_device(): lax.all_to_all(shaped, 'gz', split_axis=2, concat_axis=3, tiled=True)  19.1 us
    all_to_all x1, waiting for transfers between devices, on_device(): lax.all_to_all(shaped, 'gz', split_axis=2, concat_axis=3, tiled=True)  15.2 us
    all_to_all x1, starting transfers between devices, on_device(): lax.all_to_all(rates, 'gz', split_axis=2, concat_axis=3, tiled=True)  8.31 us
    div x10, other arithmetic, reduce_step(): -couple_up * overhead[1] / pivot  7.61 us
    all_to_all x1, starting transfers between devices, on_device(): lax.all_to_all(shaped, 'gz', split_axis=2, concat_axis=3, tiled=True)  6.51 us
    slice x12, local copies, waits for them, and re-layouts, offset_rows(): lax.slice_in_dim(values, -offset, length, axis=axis)  5.55 us
    another operation x10, other arithmetic, reduce_step(): jnp.stack([-couple_down * beneath[0] / pivot, -couple_up * overhead[1] /...  3.65 us
  transfers between devices with their start and end apart: 10, of which 9 were waited for; matrix products, arithmetic and copies ran while one was open for 5% of the time, Pallas kernels for 0%

commit v1 on v0

v1 whole, which is shorter than its diff:
```python
import functools

import jax
import jax.numpy as jnp
from jax import lax
from jax.experimental import pallas as pl
from jax.experimental.pallas import tpu as pltpu
from jax.sharding import PartitionSpec as P

STEPS = 2
TILE_ROWS = 8
TILE_LANES = 128
MESH = pl.DeviceIdType.MESH


def tendency(q, north, south, along_x, along_y, spread):
    width = q.shape[1]
    eastern = pltpu.roll(q, width - 1, 1)
    western = pltpu.roll(q, 1, 1)
    return spread * (eastern + western + north + south - 4.0 * q) - 0.5 * (
        along_x * (eastern - western) + along_y * (north - south)
    )


def join(lower, upper):
    between = lower[2] + upper[1]
    inverse = 1.0 / (lower[0] + upper[0] + between)
    to_low = lower[0] * inverse
    to_high = upper[0] * inverse
    element = (to_low * upper[0], lower[1] + to_low * between, upper[2] + to_high * between)
    return element, (to_low, to_high, inverse)


def layer_element(rate):
    return (rate, jnp.zeros_like(rate), jnp.ones_like(rate))


def kernel(
    plan,
    xy_rate,
    z_scale,
    fields,
    velocity,
    face_rate,
    out,
    present,
    speed,
    rates,
    rates_plane,
    coef0,
    held0,
    coef1,
    held1,
    coef2,
    send1,
    recv1,
    back1,
    home1,
    send2,
    recv2,
    back2,
    home2,
    send_el,
    recv_el,
    local_sem,
    halo_send,
    halo_recv,
    rate_send,
    rate_recv,
    s1_send,
    s1_recv,
    b1_send,
    b1_recv,
    s2_send,
    s2_recv,
    b2_send,
    b2_recv,
    el_send,
    el_recv,
):
    g1, g2, owners, per_field, fields_each, rows_each, gy_count = plan
    field_total, layers, rows, width = fields.shape
    halo = TILE_ROWS
    me = lax.axis_index("gz")
    my_y = lax.axis_index("gy")
    mine1 = lax.rem(me, g1)
    mine2 = lax.div(me, g1)
    upper_y = lax.rem(my_y + 1, gy_count)
    lower_y = lax.rem(my_y + gy_count - 1, gy_count)

    def plane_peer(offset):
        return lax.rem(mine1 + offset, g1)

    def plane_source(offset):
        return lax.rem(mine1 + g1 - offset, g1)

    def stack_peer(offset):
        return lax.rem(mine2 + offset, g2)

    def stack_source(offset):
        return lax.rem(mine2 + g2 - offset, g2)

    def plane_id(position):
        return {"gz": mine2 * g1 + position}

    def stack_id(position):
        return {"gz": position * g1 + mine1}

    def lanes(position):
        return pl.ds(pl.multiple_of(position * TILE_LANES, TILE_LANES), TILE_LANES)

    locals_in = [
        pltpu.make_async_copy(face_rate, rates, local_sem.at[0]),
        pltpu.make_async_copy(
            face_rate.at[:, :, lanes(mine1)], rates_plane.at[mine1], local_sem.at[1]
        ),
        pltpu.make_async_copy(fields, present.at[0, :, :, pl.ds(halo, rows)], local_sem.at[2]),
        pltpu.make_async_copy(velocity, speed.at[:, :, pl.ds(halo, rows)], local_sem.at[3]),
    ]
    for copy in locals_in:
        copy.start()

    barrier = pltpu.get_barrier_semaphore()
    for target in (lower_y, upper_y):
        pl.semaphore_signal(barrier, inc=1, device_id={"gy": target}, device_id_type=MESH)
    for offset in range(1, g1):
        pl.semaphore_signal(
            barrier, inc=1, device_id=plane_id(plane_peer(offset)), device_id_type=MESH
        )
    for offset in range(1, g2):
        pl.semaphore_signal(
            barrier, inc=1, device_id=stack_id(stack_peer(offset)), device_id_type=MESH
        )
    pl.semaphore_wait(barrier, 2 + g1 - 1 + g2 - 1)

    sent = []

    def remote(source, target, send_sem, recv_sem, device):
        copy = pltpu.make_async_remote_copy(
            src_ref=source,
            dst_ref=target,
            send_sem=send_sem,
            recv_sem=recv_sem,
            device_id=device,
            device_id_type=MESH,
        )
        return copy

    def halo_copies(source, first, target, slot):
        return [
            remote(
                source.at[:, :, pl.ds(first, halo)],
                target.at[:, :, pl.ds(halo + rows, halo)],
                halo_send.at[slot, 0],
                halo_recv.at[slot, 0],
                {"gy": lower_y},
            ),
            remote(
                source.at[:, :, pl.ds(first + rows - halo, halo)],
                target.at[:, :, pl.ds(0, halo)],
                halo_send.at[slot, 1],
                halo_recv.at[slot, 1],
                {"gy": upper_y},
            ),
        ]

    def begin(copies):
        for copy in copies:
            copy.start()
        sent.extend(copies)
        return copies

    halos = begin(halo_copies(fields, 0, present.at[0], 0))
    speed_halos = begin(halo_copies(velocity, 0, speed, STEPS))
    rate_copies = begin(
        [
            remote(
                face_rate.at[:, :, lanes(plane_peer(offset))],
                rates_plane.at[mine1],
                rate_send.at[offset - 1],
                rate_recv.at[offset - 1],
                plane_id(plane_peer(offset)),
            )
            for offset in range(1, g1)
        ]
    )

    locals_in[0].wait()

    def own_factors(f, carry):
        scale = z_scale[f]
        element = layer_element(scale * rates[0])
        for k in range(1, layers):
            element, factors = join(element, layer_element(scale * rates[k]))
            for n in range(3):
                coef0[n, k - 1, f] = factors[n]
        return carry

    lax.fori_loop(0, field_total, own_factors, 0)
    for copy in locals_in[1:]:
        copy.wait()

    def plane_factors():
        for copy in rate_copies:
            copy.wait_recv()

        def one(f, carry):
            scale = z_scale[f]
            total = None
            for i in range(g1):
                element = layer_element(scale * rates_plane[i, 0])
                for k in range(1, layers):
                    element, ignored = join(element, layer_element(scale * rates_plane[i, k]))
                if total is None:
                    total = element
                else:
                    total, factors = join(total, element)
                    for n in range(3):
                        coef1[n, i - 1, f] = factors[n]
            for n in range(3):
                for part in range(per_field):
                    cut = slice(part * rows_each, (part + 1) * rows_each)
                    send_el[f // fields_each * per_field + part, n, f % fields_each] = total[n][cut]
            return carry

        for f in range(field_total):
            one(f, 0)

    def to_owners(source, target, send_sem, recv_sem):
        copies = []
        for offset in range(1, g2):
            copies.append(
                remote(
                    source.at[lax.rem(stack_peer(offset), owners)],
                    target.at[mine2],
                    send_sem.at[offset - 1],
                    recv_sem.at[offset - 1],
                    stack_id(stack_peer(offset)),
                )
            )
        return copies

    def stack_factors():
        total = tuple(recv_el[0, n] for n in range(3))
        for g in range(1, g2):
            total, factors = join(total, tuple(recv_el[g, n] for n in range(3)))
            coef2[0, g - 1] = factors[1]
            coef2[1, g - 1] = factors[2]
        coef2[0, g2 - 1] = 1.0 / (total[0] + total[2])

    for step in range(STEPS):
        for copy in halos:
            copy.wait_recv()
        if step == 0:
            for copy in speed_halos:
                copy.wait_recv()

        def own_forward(f, carry):
            spread = xy_rate[f]
            low = None
            high = None
            inner = slice(halo, halo + rows)
            for k in range(layers):
                q = present[step, f, k]
                along_x = speed[0, k]
                along_y = speed[1, k]
                extent = q.shape[0]
                sectioned = q + tendency(
                    q, pltpu.roll(q, extent - 1, 0), pltpu.roll(q, 1, 0), along_x, along_y, spread
                )
                north = pltpu.roll(sectioned, extent - 1, 0)[inner]
                south = pltpu.roll(sectioned, 1, 0)[inner]
                middle = sectioned[inner]
                explicit = 0.5 * q[inner] + 0.5 * (
                    middle
                    + tendency(middle, north, south, along_x[inner], along_y[inner], spread)
                )
                if k == 0:
                    high = explicit
                else:
                    held0[k - 1, f] = high
                    share = coef0[0, k - 1, f] * high
                    low = share if low is None else low + share
                    high = explicit + coef0[1, k - 1, f] * high
            for c in range(g1):
                cut = slice(c * TILE_LANES, (c + 1) * TILE_LANES)
                send1[step, c, 0, f] = low[:, cut]
                send1[step, c, 1, f] = high[:, cut]
            return carry

        lax.fori_loop(0, field_total, own_forward, 0)

        out1 = begin(
            [
                remote(
                    send1.at[step, plane_peer(offset)],
                    recv1.at[step, mine1],
                    s1_send.at[step, offset - 1],
                    s1_recv.at[step, offset - 1],
                    plane_id(plane_peer(offset)),
                )
                for offset in range(1, g1)
            ]
        )
        recv1[step, mine1] = send1[step, mine1]
        if step == 0:
            plane_factors()
            elements = begin(to_owners(send_el, recv_el, el_send, el_recv))
            recv_el[mine2] = send_el[lax.rem(mine2, owners)]
        for copy in out1:
            copy.wait_recv()

        low = recv1[step, 0, 0]
        high = recv1[step, 0, 1]
        for i in range(1, g1):
            meeting = high + recv1[step, i, 0]
            held1[i - 1] = meeting
            low = low + coef1[0, i - 1] * meeting
            high = recv1[step, i, 1] + coef1[1, i - 1] * meeting
        for o in range(owners):
            field0 = o // per_field * fields_each
            row0 = o % per_field * rows_each
            cut = (slice(field0, field0 + fields_each), slice(row0, row0 + rows_each))
            send2[step, o, 0] = low[cut]
            send2[step, o, 1] = high[cut]
        out2 = begin(to_owners(send2.at[step], recv2.at[step], s2_send.at[step], s2_recv.at[step]))
        recv2[step, mine2] = send2[step, lax.rem(mine2, owners)]
        if step == 0:
            for copy in elements:
                copy.wait_recv()
            stack_factors()
        for copy in out2:
            copy.wait_recv()

        high = recv2[step, 0, 1]
        meetings = []
        for g in range(1, g2):
            meeting = high + recv2[step, g, 0]
            meetings.append(meeting)
            high = recv2[step, g, 1] + coef2[0, g - 1] * meeting
        value = high * coef2[0, g2 - 1]
        back2[step, g2 - 1, 1] = value
        for g in range(g2 - 1, 0, -1):
            value = meetings[g - 1] * coef2[1, g - 1] + coef2[0, g - 1] * value
            back2[step, g, 0] = value
            back2[step, g - 1, 1] = value
        back2[step, 0, 0] = jnp.zeros_like(value)
        home = []
        for offset in range(1, g2):
            home.append(
                remote(
                    back2.at[step, stack_peer(offset)],
                    home2.at[step, mine2],
                    b2_send.at[step, offset - 1],
                    b2_recv.at[step, offset - 1],
                    stack_id(stack_peer(offset)),
                )
            )
        begin(home)
        home2[step, mine2] = back2[step, mine2]
        for copy in home:
            copy.wait_recv()

        for o in range(owners):
            field0 = o // per_field * fields_each
            row0 = o % per_field * rows_each
            cut = (slice(field0, field0 + fields_each), slice(row0, row0 + rows_each))
            base = home2[step, o, 0]
            value = home2[step, o, 1]
            back1[(step, g1 - 1, 1) + cut] = value
            for i in range(g1 - 1, 0, -1):
                value = (
                    held1[(i - 1,) + cut] * coef1[(2, i - 1) + cut]
                    + coef1[(0, i - 1) + cut] * base
                    + coef1[(1, i - 1) + cut] * value
                )
                back1[(step, i, 0) + cut] = value
                back1[(step, i - 1, 1) + cut] = value
            back1[(step, 0, 0) + cut] = base
        home = begin(
            [
                remote(
                    back1.at[step, plane_peer(offset)],
                    home1.at[step, mine1],
                    b1_send.at[step, offset - 1],
                    b1_recv.at[step, offset - 1],
                    plane_id(plane_peer(offset)),
                )
                for offset in range(1, g1)
            ]
        )
        home1[step, mine1] = back1[step, mine1]
        for copy in home:
            copy.wait_recv()

        def own_backward(f, carry):
            for c in range(g1):
                cut = slice(c * TILE_LANES, (c + 1) * TILE_LANES)
                base = home1[step, c, 0, f]
                value = home1[step, c, 1, f]
                for k in range(layers - 1, -1, -1):
                    if k < layers - 1:
                        value = (
                            held0[k, f, :, cut] * coef0[2, k, f, :, cut]
                            + coef0[0, k, f, :, cut] * base
                            + coef0[1, k, f, :, cut] * value
                        )
                    if step == STEPS - 1:
                        out[f, k, :, cut] = value
                    else:
                        present[step + 1, f, k, halo : halo + rows, cut] = value
            return carry

        lax.fori_loop(0, field_total, own_backward, 0)
        if step < STEPS - 1:
            halos = begin(halo_copies(present.at[step + 1], halo, present.at[step + 1], step + 1))

    for copy in sent:
        copy.wait_send()


def on_device(fields, velocity, face_rate, xy_rate, z_scale):
    gz_count = lax.axis_size("gz")
    gy_count = lax.axis_size("gy")
    field_total, layers, rows, width = fields.shape
    g1 = width // TILE_LANES
    g2 = gz_count // g1
    owners = min(g2, field_total * rows // TILE_ROWS)
    per_field = max(1, owners // field_total)
    fields_each = max(1, field_total // owners)
    rows_each = rows // per_field
    plan = (g1, g2, owners, per_field, fields_each, rows_each, gy_count)
    extent = rows + 2 * TILE_ROWS
    share1 = (field_total, rows, TILE_LANES)
    share2 = (fields_each, rows_each, TILE_LANES)
    vmem = lambda *shape: pltpu.VMEM(shape, jnp.float32)
    dma = lambda *shape: pltpu.SemaphoreType.DMA(shape)
    return pl.pallas_call(
        functools.partial(kernel, plan),
        out_shape=jax.ShapeDtypeStruct(fields.shape, jnp.float32),
        in_specs=[pl.BlockSpec(memory_space=pltpu.SMEM)] * 2
        + [pl.BlockSpec(memory_space=pl.ANY)] * 3,
        out_specs=pl.BlockSpec(memory_space=pltpu.VMEM),
        scratch_shapes=[
            vmem(STEPS, field_total, layers, extent, width),
            vmem(2, layers, extent, width),
            vmem(layers, rows, width),
            vmem(g1, layers, rows, TILE_LANES),
            vmem(3, layers - 1, field_total, rows, width),
            vmem(layers - 1, field_total, rows, width),
            vmem(3, g1 - 1, *share1),
            vmem(g1 - 1, *share1),
            vmem(2, g2, *share2),
            vmem(STEPS, g1, 2, *share1),
            vmem(STEPS, g1, 2, *share1),
            vmem(STEPS, g1, 2, *share1),
            vmem(STEPS, g1, 2, *share1),
            vmem(STEPS, owners, 2, *share2),
            vmem(STEPS, g2, 2, *share2),
            vmem(STEPS, g2, 2, *share2),
            vmem(STEPS, g2, 2, *share2),
            vmem(owners, 3, *share2),
            vmem(g2, 3, *share2),
            dma(4),
            dma(STEPS + 1, 2),
            dma(STEPS + 1, 2),
            dma(g1 - 1),
            dma(g1 - 1),
            dma(STEPS, g1 - 1),
            dma(STEPS, g1 - 1),
            dma(STEPS, g1 - 1),
            dma(STEPS, g1 - 1),
            dma(STEPS, g2 - 1),
            dma(STEPS, g2 - 1),
            dma(STEPS, g2 - 1),
            dma(STEPS, g2 - 1),
            dma(g2 - 1),
            dma(g2 - 1),
        ],
        compiler_params=pltpu.CompilerParams(
            collective_id=0, has_side_effects=True, vmem_limit_bytes=40 * 1024 * 1024
        ),
        cost_estimate=pl.CostEstimate(
            flops=400 * fields.size, bytes_accessed=16 * fields.size, transcendentals=0
        ),
    )(xy_rate, z_scale, fields, velocity, face_rate)


def solution(mesh):
    in_specs = (P(None, "gz", "gy", None), P(None, "gz", "gy", None), P("gz", "gy", None), P(), P())
    out_specs = P(None, "gz", "gy", None)
    return jax.shard_map(
        on_device, mesh=mesh, in_specs=in_specs, out_specs=out_specs, check_vma=False
    )
```

time: 121 us -> 51 us (0.42)
  blocking collectives: 55.4 us -> 0 us
  Pallas kernels: 0 us -> 45.8 us
  waiting for transfers between devices: 18.2 us -> 0 us
  other arithmetic: 17.8 us -> 0 us
  starting transfers between devices: 17.1 us -> 0 us
  local copies, waits for them, and re-layouts: 11.9 us -> 5 us
    all_to_all x3 -> x0, blocking collectives: 55.4 us -> none  [the longest x2 36.4 us: on_device(): lax.all_to_all(solved, 'gz', split_axis=3, concat_axis=2, tiled=True)]
    pallas_call x0 -> x1, Pallas kernels: none -> 45.8 us  [on_device(): pl.pallas_call(functools.partial(kernel, plan), out_shape=jax.ShapeDtypeS...]
    all_to_all x2 -> x0, waiting for transfers between devices: 15.6 us -> none  [the longest x1 15.2 us: on_device(): lax.all_to_all(shaped, 'gz', split_axis=2, concat_axis=3, tiled=True)]
    all_to_all x2 -> x0, starting transfers between devices: 14.8 us -> none  [the longest x1 8.31 us: on_device(): lax.all_to_all(rates, 'gz', split_axis=2, concat_axis=3, tiled=True)]
    div x13 -> x0, other arithmetic: 8.63 us -> none  [the longest x10 7.61 us: reduce_step(): -couple_up * overhead[1] / pivot]
    slice x25 -> x0, local copies, waits for them, and re-layouts: 7.49 us -> none  [the longest x12 5.55 us: offset_rows(): lax.slice_in_dim(values, -offset, length, axis=axis)]
    another operation x13 -> x0, other arithmetic: 4.83 us -> none  [the longest x10 3.65 us: reduce_step(): jnp.stack([-couple_down * beneath[0] / pivot, -couple_up * overhead[1] /...]
    ppermute x8 -> x0, waiting for transfers between devices: 2.69 us -> none  [the longest x4 1.7 us: with_halo(): lax.ppermute(lax.slice_in_dim(block, 0, width, axis=dim), axis, backward)]
  transfers between devices with their start and end apart: 10 -> 0, of which waited for: 9 -> 0; matrix products, arithmetic and copies ran while one was open for 5% -> 0% of each run, Pallas kernels for 0% -> 0%
where the time goes in v1:
time: 51 us; the launch traced here: 50.8 us
  Pallas kernels  45.8 us (90%)
  local copies, waits for them, and re-layouts  5 us (10%)
    pallas_call x1, Pallas kernels, on_device(): pl.pallas_call(functools.partial(kernel, plan), out_shape=jax.ShapeDtypeS...  45.8 us
    unnamed x11, local copies, waits for them, and re-layouts  5 us

profile of v1, /device:TPU:0, one launch (start us, length us, event | category | flops | bytes accessed | tf_op | source)
XLA Modules:
  0.0 50.8 jit_solution(6165410481386739104)
XLA Ops:
  0.0 0.0 copy-start
  0.0 1.0 %copy-done = f32[4,4,16,512]{3,2,1,0:T(8,128)S(1)} copy-done((f32[4,4,16,512]{3,2,1,0:T(8,128)S(1)}, f32[4,4,16,512]{3,2,1,0:T(8,128)}, u32[]{:S(2)}) %copy-start) | copy-done | bytes 524312
  1.0 0.0 copy-start.1
  1.0 0.9 %copy-done.1 = f32[2,4,16,512]{3,2,1,0:T(8,128)S(1)} copy-done((f32[2,4,16,512]{3,2,1,0:T(8,128)S(1)}, f32[2,4,16,512]{3,2,1,0:T(8,128)}, u32[]{:S(2)}) %copy-start.1) | copy-done | bytes 262168
  2.0 0.0 copy-start.2
  2.0 0.9 %copy-done.2 = f32[4,16,512]{2,1,0:T(8,128)S(1)} copy-done((f32[4,16,512]{2,1,0:T(8,128)S(1)}, f32[4,16,512]{2,1,0:T(8,128)}, u32[]{:S(2)}) %copy-start.2) | copy-done | bytes 131096
  2.9 0.0 copy-start.3
  2.9 0.7 %copy-done.3 = f32[4]{0:T(128)S(1)} copy-done((f32[4]{0:T(128)S(1)}, f32[4]{0:T(128)}, u32[]{:S(2)}) %copy-start.3) | copy-done | bytes 40
  3.6 0.0 copy-start.4
  3.6 0.7 %copy-done.4 = f32[4]{0:T(128)S(1)} copy-done((f32[4]{0:T(128)S(1)}, f32[4]{0:T(128)}, u32[]{:S(2)}) %copy-start.4) | copy-done | bytes 40
  4.2 45.8 %shard_map.55 = f32[4,4,16,512]{3,2,1,0:T(8,128)S(1)} custom-call(f32[4]{0:T(128)S(1)} %copy-done.3, f32[4]{0:T(128)S(1)} %copy-done.4, f32[4,4,16,512]{3,2,1,0:T(8,128)S(1)} %copy-done, f32[2,4,16,512]{3,2,1,0:T(8,128)S(1)} %copy-done.1, f32[4,16,512]{2,1,0:T(8,128)S(1)} %copy-done.2), custom_call_target="tpu_custom_call" | custom-call | flops 52428800 | bytes 2097152 | tf_op jit(solution)/shard_map/pallas_call | solution.py:438
  50.0 0.8 %copy.7 = f32[4,4,16,512]{3,2,1,0:T(8,128)} copy(f32[4,4,16,512]{3,2,1,0:T(8,128)S(1)} %shard_map.55) | data formatting | bytes 1048576
Async XLA Ops:
  0.0 1.0 %copy-start = (f32[4,4,16,512]{3,2,1,0:T(8,128)S(1)}, f32[4,4,16,512]{3,2,1,0:T(8,128)}, u32[]{:S(2)}) copy-start(f32[4,4,16,512]{3,2,1,0:T(8,128)} %fields.1) | copy-start | bytes 1572868
  1.0 0.9 %copy-start.1 = (f32[2,4,16,512]{3,2,1,0:T(8,128)S(1)}, f32[2,4,16,512]{3,2,1,0:T(8,128)}, u32[]{:S(2)}) copy-start(f32[2,4,16,512]{3,2,1,0:T(8,128)} %velocity.1) | copy-start | bytes 786436
  2.0 0.9 %copy-start.2 = (f32[4,16,512]{2,1,0:T(8,128)S(1)}, f32[4,16,512]{2,1,0:T(8,128)}, u32[]{:S(2)}) copy-start(f32[4,16,512]{2,1,0:T(8,128)} %face_rate.1) | copy-start | bytes 393220
  2.9 0.7 %copy-start.3 = (f32[4]{0:T(128)S(1)}, f32[4]{0:T(128)}, u32[]{:S(2)}) copy-start(f32[4]{0:T(128)} %xy_rate.1) | copy-start | bytes 52
  3.6 0.7 %copy-start.4 = (f32[4]{0:T(128)S(1)}, f32[4]{0:T(128)}, u32[]{:S(2)}) copy-start(f32[4]{0:T(128)} %z_scale.1) | copy-start | bytes 52

commit v2 on v0

v2 whole, which is shorter than its diff:
```python
import functools

import jax
import jax.numpy as jnp
from jax import lax
from jax.experimental import pallas as pl
from jax.experimental.pallas import tpu as pltpu
from jax.sharding import PartitionSpec as P

STEPS = 2
TILE_ROWS = 8
TILE_LANES = 128
MESH = pl.DeviceIdType.MESH


def stencil(q, north, south, weights):
    width = q.shape[1]
    east, west, up, down, centre = weights
    eastern = pltpu.roll(q, width - 1, 1)
    western = pltpu.roll(q, 1, 1)
    return (east * eastern + west * western) + (up * north + down * south) + centre * q


def join(lower, upper):
    between = lower[2] + upper[1]
    inverse = 1.0 / (lower[0] + upper[0] + between)
    to_low = lower[0] * inverse
    to_high = upper[0] * inverse
    element = (to_low * upper[0], lower[1] + to_low * between, upper[2] + to_high * between)
    return element, (to_low, to_high, inverse)


def layer_element(rate):
    return (rate, jnp.zeros_like(rate), jnp.ones_like(rate))


def kernel(
    plan,
    xy_hbm,
    z_hbm,
    fields,
    velocity,
    face_rate,
    out,
    xy_rate,
    z_scale,
    present,
    speed,
    rates,
    rates_plane,
    coef0,
    held0,
    coef1,
    held1,
    coef2,
    send1,
    recv1,
    back1,
    home1,
    send2,
    recv2,
    back2,
    home2,
    send_el,
    recv_el,
    local_sem,
    field_sem,
    halo_send,
    halo_recv,
    speed_send,
    speed_recv,
    rate_send,
    rate_recv,
    s1_send,
    s1_recv,
    b1_send,
    b1_recv,
    s2_send,
    s2_recv,
    b2_send,
    b2_recv,
    el_send,
    el_recv,
):
    g1, g2, owners, per_field, fields_each, rows_each, gy_count = plan
    field_total, layers, rows, width = fields.shape
    halo = TILE_ROWS
    me = lax.axis_index("gz")
    my_y = lax.axis_index("gy")
    mine1 = lax.rem(me, g1)
    mine2 = lax.div(me, g1)
    upper_y = lax.rem(my_y + 1, gy_count)
    lower_y = lax.rem(my_y + gy_count - 1, gy_count)

    def plane_peer(offset):
        return lax.rem(mine1 + offset, g1)

    def stack_peer(offset):
        return lax.rem(mine2 + offset, g2)

    def plane_id(position):
        return {"gz": mine2 * g1 + position}

    def stack_id(position):
        return {"gz": position * g1 + mine1}

    def lanes(position):
        return pl.ds(pl.multiple_of(position * TILE_LANES, TILE_LANES), TILE_LANES)

    def each_field(body):
        def step_body(f, carry):
            body(f)
            return carry

        lax.fori_loop(0, field_total, step_body, 0)

    def remote(source, target, send_sem, recv_sem, device):
        return pltpu.make_async_remote_copy(
            src_ref=source,
            dst_ref=target,
            send_sem=send_sem,
            recv_sem=recv_sem,
            device_id=device,
            device_id_type=MESH,
        )

    def field_in(f):
        return pltpu.make_async_copy(
            fields.at[f], present.at[0, f, :, pl.ds(0, rows)], field_sem.at[f]
        )

    locals_in = [
        pltpu.make_async_copy(z_hbm, z_scale, local_sem.at[0]),
        pltpu.make_async_copy(xy_hbm, xy_rate, local_sem.at[1]),
        pltpu.make_async_copy(face_rate, rates, local_sem.at[2]),
        pltpu.make_async_copy(velocity, speed.at[:, :, pl.ds(0, rows)], local_sem.at[3]),
        pltpu.make_async_copy(
            face_rate.at[:, :, lanes(mine1)], rates_plane.at[mine1], local_sem.at[4]
        ),
    ]
    for copy in locals_in:
        copy.start()
    each_field(lambda f: field_in(f).start())

    barrier = pltpu.get_barrier_semaphore()
    for target in (lower_y, upper_y):
        pl.semaphore_signal(barrier, inc=1, device_id={"gy": target}, device_id_type=MESH)
    for offset in range(1, g1):
        pl.semaphore_signal(
            barrier, inc=1, device_id=plane_id(plane_peer(offset)), device_id_type=MESH
        )
    for offset in range(1, g2):
        pl.semaphore_signal(
            barrier, inc=1, device_id=stack_id(stack_peer(offset)), device_id_type=MESH
        )
    pl.semaphore_wait(barrier, 2 + g1 - 1 + g2 - 1)

    def halo_pair(source, target, send_sem, recv_sem):
        return [
            remote(
                source.at[..., pl.ds(0, halo), :],
                target.at[..., pl.ds(rows, halo), :],
                send_sem.at[0],
                recv_sem.at[0],
                {"gy": lower_y},
            ),
            remote(
                source.at[..., pl.ds(rows - halo, halo), :],
                target.at[..., pl.ds(rows + halo, halo), :],
                send_sem.at[1],
                recv_sem.at[1],
                {"gy": upper_y},
            ),
        ]

    def halos(step, f):
        source = fields.at[f] if step == 0 else present.at[step, f]
        return halo_pair(
            source, present.at[step, f], halo_send.at[step, f], halo_recv.at[step, f]
        )

    def rate_copy(offset):
        return remote(
            face_rate.at[:, :, lanes(plane_peer(offset))],
            rates_plane.at[mine1],
            rate_send.at[offset - 1],
            rate_recv.at[offset - 1],
            plane_id(plane_peer(offset)),
        )

    def out1(step, f, offset):
        return remote(
            send1.at[step, plane_peer(offset), f],
            recv1.at[step, mine1, f],
            s1_send.at[step, f, offset - 1],
            s1_recv.at[step, f, offset - 1],
            plane_id(plane_peer(offset)),
        )

    def in1(step, f, offset):
        return remote(
            back1.at[step, plane_peer(offset), f],
            home1.at[step, mine1, f],
            b1_send.at[step, f, offset - 1],
            b1_recv.at[step, f, offset - 1],
            plane_id(plane_peer(offset)),
        )

    def owner_of(f, part):
        return lax.div(f, fields_each) * per_field + part

    def out2(step, f, part):
        owner = owner_of(f, part)
        inner = lax.rem(f, fields_each)
        return remote(
            send2.at[step, f, part],
            recv2.at[step, inner, mine2],
            s2_send.at[step, f, part],
            s2_recv.at[step, inner, mine2],
            stack_id(owner),
        )

    def el_out(f, part):
        owner = owner_of(f, part)
        inner = lax.rem(f, fields_each)
        return remote(
            send_el.at[f, part],
            recv_el.at[inner, mine2],
            el_send.at[f, part],
            el_recv.at[inner, mine2],
            stack_id(owner),
        )

    def arrival2(buffer, source_of, recv_sem, inner, source):
        return remote(source_of, buffer.at[inner, source], recv_sem, recv_sem, stack_id(source))

    my_first = lax.div(mine2, per_field) * fields_each
    my_part = lax.rem(mine2, per_field)

    def in2(step, inner, offset):
        f = my_first + inner
        peer = stack_peer(offset)
        return remote(
            back2.at[step, inner, peer],
            home2.at[step, f, my_part],
            b2_send.at[step, inner, offset - 1],
            b2_recv.at[step, f, my_part],
            stack_id(peer),
        )

    def home_arrival(step, f, part):
        return remote(
            home2.at[step, f, part],
            home2.at[step, f, part],
            b2_recv.at[step, f, part],
            b2_recv.at[step, f, part],
            stack_id(owner_of(f, part)),
        )

    def as_owner(body):
        if owners == g2:
            body()
        else:
            pl.when(mine2 < owners)(body)

    def parts(f, same, other):
        for part in range(per_field):
            own = owner_of(f, part) == mine2
            if same is not None:
                pl.when(own)(functools.partial(same, part))
            pl.when(jnp.logical_not(own))(functools.partial(other, part))

    def rows_of(part):
        return slice(part * rows_each, (part + 1) * rows_each)

    speed_halos = halo_pair(velocity, speed, speed_send, speed_recv)
    for copy in speed_halos:
        copy.start()

    def start_halos(f):
        for copy in halos(0, f):
            copy.start()

    each_field(start_halos)
    for offset in range(1, g1):
        rate_copy(offset).start()

    for copy in locals_in[:3]:
        copy.wait()

    def own_factors(f):
        scale = z_scale[f]
        element = layer_element(scale * rates[0])
        for k in range(1, layers):
            element, factors = join(element, layer_element(scale * rates[k]))
            for n in range(3):
                coef0[n, k - 1, f] = factors[n]

    each_field(own_factors)

    def ring(block):
        place = lax.broadcasted_iota(jnp.int32, (halo, width), 0)
        edge = jnp.where(
            place < halo // 2, block[rows : rows + halo], block[rows + halo : rows + 2 * halo]
        )
        return jnp.concatenate([block[:rows], edge], axis=0)

    for copy in locals_in[3:]:
        copy.wait()
    for copy in speed_halos:
        copy.wait_recv()
    for n in range(2):
        for k in range(layers):
            speed[n, k, : rows + halo] = 0.5 * ring(speed[n, k])

    def plane_factors(f):
        scale = z_scale[f]
        total = None
        for i in range(g1):
            element = layer_element(scale * rates_plane[i, 0])
            for k in range(1, layers):
                element, ignored = join(element, layer_element(scale * rates_plane[i, k]))
            if total is None:
                total = element
            else:
                total, factors = join(total, element)
                for n in range(3):
                    coef1[n, i - 1, f] = factors[n]
        inner = lax.rem(f, fields_each)
        for part in range(per_field):
            for n in range(3):
                send_el[f, part, n] = total[n][rows_of(part)]

        def same(part):
            recv_el[inner, mine2] = send_el[f, part]

        parts(f, same, lambda part: el_out(f, part).start())

    def stack_factors():
        for inner in range(fields_each):
            for offset in range(1, g2):
                source = stack_peer(offset)
                arrival2(
                    recv_el, send_el.at[0, 0], el_recv.at[inner, source], inner, source
                ).wait_recv()
            total = tuple(recv_el[inner, 0, n] for n in range(3))
            for g in range(1, g2):
                total, factors = join(total, tuple(recv_el[inner, g, n] for n in range(3)))
                coef2[inner, 0, g - 1] = factors[1]
                coef2[inner, 1, g - 1] = factors[2]
            coef2[inner, 0, g2 - 1] = 1.0 / (total[0] + total[2])

    def own_forward(step, f):
        if step == 0:
            field_in(f).wait()
        for copy in halos(step, f):
            copy.wait_recv()
        spread = xy_rate[f]
        centre = 1.0 - 4.0 * spread
        low = None
        high = None
        extent = rows + halo
        for k in range(layers):
            q = ring(present[step, f, k])
            along_x = speed[0, k, :extent]
            along_y = speed[1, k, :extent]
            weights = (
                spread - along_x,
                spread + along_x,
                spread - along_y,
                spread + along_y,
                centre,
            )
            sectioned = stencil(q, pltpu.roll(q, extent - 1, 0), pltpu.roll(q, 1, 0), weights)
            north = pltpu.roll(sectioned, extent - 1, 0)[:rows]
            south = pltpu.roll(sectioned, 1, 0)[:rows]
            inner_weights = tuple(w[:rows] for w in weights[:4]) + (centre,)
            explicit = 0.5 * (
                q[:rows] + stencil(sectioned[:rows], north, south, inner_weights)
            )
            if k == 0:
                high = explicit
            else:
                held0[k - 1, f] = high
                share = coef0[0, k - 1, f] * high
                low = share if low is None else low + share
                high = explicit + coef0[1, k - 1, f] * high
        for c in range(g1):
            cut = slice(c * TILE_LANES, (c + 1) * TILE_LANES)
            send1[step, c, f, 0] = low[:, cut]
            send1[step, c, f, 1] = high[:, cut]
        for offset in range(1, g1):
            out1(step, f, offset).start()
        recv1[step, mine1, f] = send1[step, mine1, f]

    def plane_forward(step, f):
        for offset in range(1, g1):
            out1(step, f, offset).wait_recv()
        low = recv1[step, 0, f, 0]
        high = recv1[step, 0, f, 1]
        for i in range(1, g1):
            meeting = high + recv1[step, i, f, 0]
            held1[i - 1, f] = meeting
            low = low + coef1[0, i - 1, f] * meeting
            high = recv1[step, i, f, 1] + coef1[1, i - 1, f] * meeting
        for part in range(per_field):
            send2[step, f, part, 0] = low[rows_of(part)]
            send2[step, f, part, 1] = high[rows_of(part)]
        inner = lax.rem(f, fields_each)

        def same(part):
            recv2[step, inner, mine2] = send2[step, f, part]

        parts(f, same, lambda part: out2(step, f, part).start())

    def stack_solve(step):
        for inner in range(fields_each):
            for offset in range(1, g2):
                source = stack_peer(offset)
                arrival2(
                    recv2.at[step],
                    send2.at[step, 0, 0],
                    s2_recv.at[step, inner, source],
                    inner,
                    source,
                ).wait_recv()
            high = recv2[step, inner, 0, 1]
            meetings = []
            for g in range(1, g2):
                meeting = high + recv2[step, inner, g, 0]
                meetings.append(meeting)
                high = recv2[step, inner, g, 1] + coef2[inner, 0, g - 1] * meeting
            value = high * coef2[inner, 0, g2 - 1]
            back2[step, inner, g2 - 1, 1] = value
            for g in range(g2 - 1, 0, -1):
                value = (
                    meetings[g - 1] * coef2[inner, 1, g - 1] + coef2[inner, 0, g - 1] * value
                )
                back2[step, inner, g, 0] = value
                back2[step, inner, g - 1, 1] = value
            back2[step, inner, 0, 0] = jnp.zeros_like(value)
            for offset in range(1, g2):
                in2(step, inner, offset).start()
            home2[step, my_first + inner, my_part] = back2[step, inner, mine2]

    def plane_backward(step, f):
        parts(f, None, lambda part: home_arrival(step, f, part).wait_recv())
        for part in range(per_field):
            cut = rows_of(part)
            base = home2[step, f, part, 0]
            value = home2[step, f, part, 1]
            back1[step, g1 - 1, f, 1, cut] = value
            for i in range(g1 - 1, 0, -1):
                value = (
                    held1[i - 1, f, cut] * coef1[2, i - 1, f, cut]
                    + coef1[0, i - 1, f, cut] * base
                    + coef1[1, i - 1, f, cut] * value
                )
                back1[step, i, f, 0, cut] = value
                back1[step, i - 1, f, 1, cut] = value
            back1[step, 0, f, 0, cut] = base
        for offset in range(1, g1):
            in1(step, f, offset).start()
        home1[step, mine1, f] = back1[step, mine1, f]

    def own_backward(step, f):
        for offset in range(1, g1):
            in1(step, f, offset).wait_recv()
        for c in range(g1):
            cut = slice(c * TILE_LANES, (c + 1) * TILE_LANES)
            base = home1[step, c, f, 0]
            value = home1[step, c, f, 1]
            for k in range(layers - 1, -1, -1):
                if k < layers - 1:
                    value = (
                        held0[k, f, :, cut] * coef0[2, k, f, :, cut]
                        + coef0[0, k, f, :, cut] * base
                        + coef0[1, k, f, :, cut] * value
                    )
                if step == STEPS - 1:
                    out[f, k, :, cut] = value
                else:
                    present[step + 1, f, k, :rows, cut] = value
        if step < STEPS - 1:
            for copy in halos(step + 1, f):
                copy.start()

    for step in range(STEPS):
        each_field(functools.partial(own_forward, step))
        if step == 0:
            for offset in range(1, g1):
                rate_copy(offset).wait_recv()
            each_field(plane_factors)
        each_field(functools.partial(plane_forward, step))
        if step == 0:
            as_owner(stack_factors)
        as_owner(functools.partial(stack_solve, step))
        each_field(functools.partial(plane_backward, step))
        each_field(functools.partial(own_backward, step))

    for copy in speed_halos:
        copy.wait_send()
    for offset in range(1, g1):
        rate_copy(offset).wait_send()
    each_field(lambda f: parts(f, None, lambda part: el_out(f, part).wait_send()))
    for step in range(STEPS):

        def sent(f, step=step):
            for copy in halos(step, f):
                copy.wait_send()
            for offset in range(1, g1):
                out1(step, f, offset).wait_send()
                in1(step, f, offset).wait_send()
            parts(f, None, lambda part: out2(step, f, part).wait_send())

        def sent_back(step=step):
            for inner in range(fields_each):
                for offset in range(1, g2):
                    in2(step, inner, offset).wait_send()

        each_field(sent)
        as_owner(sent_back)


def on_device(fields, velocity, face_rate, xy_rate, z_scale):
    gz_count = lax.axis_size("gz")
    gy_count = lax.axis_size("gy")
    field_total, layers, rows, width = fields.shape
    g1 = width // TILE_LANES
    g2 = gz_count // g1
    owners = min(g2, field_total * rows // TILE_ROWS)
    per_field = max(1, owners // field_total)
    fields_each = max(1, field_total // owners)
    rows_each = rows // per_field
    plan = (g1, g2, owners, per_field, fields_each, rows_each, gy_count)
    extent = rows + 2 * TILE_ROWS
    share1 = (rows, TILE_LANES)
    share2 = (rows_each, TILE_LANES)
    vmem = lambda *shape: pltpu.VMEM(shape, jnp.float32)
    dma = lambda *shape: pltpu.SemaphoreType.DMA(shape)
    return pl.pallas_call(
        functools.partial(kernel, plan),
        out_shape=jax.ShapeDtypeStruct(fields.shape, jnp.float32),
        in_specs=[pl.BlockSpec(memory_space=pl.ANY)] * 5,
        out_specs=pl.BlockSpec(memory_space=pltpu.VMEM),
        scratch_shapes=[
            pltpu.SMEM((field_total,), jnp.float32),
            pltpu.SMEM((field_total,), jnp.float32),
            vmem(STEPS, field_total, layers, extent, width),
            vmem(2, layers, extent, width),
            vmem(layers, rows, width),
            vmem(g1, layers, rows, TILE_LANES),
            vmem(3, layers - 1, field_total, rows, width),
            vmem(layers - 1, field_total, rows, width),
            vmem(3, g1 - 1, field_total, *share1),
            vmem(g1 - 1, field_total, *share1),
            vmem(fields_each, 2, g2, *share2),
            vmem(STEPS, g1, field_total, 2, *share1),
            vmem(STEPS, g1, field_total, 2, *share1),
            vmem(STEPS, g1, field_total, 2, *share1),
            vmem(STEPS, g1, field_total, 2, *share1),
            vmem(STEPS, field_total, per_field, 2, *share2),
            vmem(STEPS, fields_each, g2, 2, *share2),
            vmem(STEPS, fields_each, g2, 2, *share2),
            vmem(STEPS, field_total, per_field, 2, *share2),
            vmem(field_total, per_field, 3, *share2),
            vmem(fields_each, g2, 3, *share2),
            dma(5),
            dma(field_total),
            dma(STEPS, field_total, 2),
            dma(STEPS, field_total, 2),
            dma(2),
            dma(2),
            dma(g1 - 1),
            dma(g1 - 1),
            dma(STEPS, field_total, g1 - 1),
            dma(STEPS, field_total, g1 - 1),
            dma(STEPS, field_total, g1 - 1),
            dma(STEPS, field_total, g1 - 1),
            dma(STEPS, field_total, per_field),
            dma(STEPS, fields_each, g2),
            dma(STEPS, fields_each, g2 - 1),
            dma(STEPS, field_total, per_field),
            dma(field_total, per_field),
            dma(fields_each, g2),
        ],
        compiler_params=pltpu.CompilerParams(
            collective_id=0, has_side_effects=True, vmem_limit_bytes=60 * 1024 * 1024
        ),
        cost_estimate=pl.CostEstimate(
            flops=400 * fields.size, bytes_accessed=16 * fields.size, transcendentals=0
        ),
    )(xy_rate, z_scale, fields, velocity, face_rate)


def solution(mesh):
    in_specs = (P(None, "gz", "gy", None), P(None, "gz", "gy", None), P("gz", "gy", None), P(), P())
    out_specs = P(None, "gz", "gy", None)
    return jax.shard_map(
        on_device, mesh=mesh, in_specs=in_specs, out_specs=out_specs, check_vma=False
    )
```

time: 121 us -> 43.2 us (0.36)
  blocking collectives: 55.4 us -> 0 us
  Pallas kernels: 0 us -> 41.1 us
  waiting for transfers between devices: 18.2 us -> 0 us
  other arithmetic: 17.8 us -> 0 us
  starting transfers between devices: 17.1 us -> 0 us
  local copies, waits for them, and re-layouts: 11.9 us -> 1.88 us
    all_to_all x3 -> x0, blocking collectives: 55.4 us -> none  [the longest x2 36.4 us: on_device(): lax.all_to_all(solved, 'gz', split_axis=3, concat_axis=2, tiled=True)]
    pallas_call x0 -> x1, Pallas kernels: none -> 41.1 us  [on_device(): pl.pallas_call(functools.partial(kernel, plan), out_shape=jax.ShapeDtypeS...]
    all_to_all x2 -> x0, waiting for transfers between devices: 15.6 us -> none  [the longest x1 15.2 us: on_device(): lax.all_to_all(shaped, 'gz', split_axis=2, concat_axis=3, tiled=True)]
    all_to_all x2 -> x0, starting transfers between devices: 14.8 us -> none  [the longest x1 8.31 us: on_device(): lax.all_to_all(rates, 'gz', split_axis=2, concat_axis=3, tiled=True)]
    div x13 -> x0, other arithmetic: 8.63 us -> none  [the longest x10 7.61 us: reduce_step(): -couple_up * overhead[1] / pivot]
    slice x25 -> x0, local copies, waits for them, and re-layouts: 7.49 us -> none  [the longest x12 5.55 us: offset_rows(): lax.slice_in_dim(values, -offset, length, axis=axis)]
    another operation x13 -> x0, other arithmetic: 4.83 us -> none  [the longest x10 3.65 us: reduce_step(): jnp.stack([-couple_down * beneath[0] / pivot, -couple_up * overhead[1] /...]
    ppermute x8 -> x0, waiting for transfers between devices: 2.69 us -> none  [the longest x4 1.7 us: with_halo(): lax.ppermute(lax.slice_in_dim(block, 0, width, axis=dim), axis, backward)]
  transfers between devices with their start and end apart: 10 -> 0, of which waited for: 9 -> 0; matrix products, arithmetic and copies ran while one was open for 5% -> 0% of each run, Pallas kernels for 0% -> 0%
where the time goes in v2:
time: 43.2 us; the launch traced here: 43 us
  Pallas kernels  41.1 us (95%)
  local copies, waits for them, and re-layouts  1.88 us (4%)
    pallas_call x1, Pallas kernels, on_device(): pl.pallas_call(functools.partial(kernel, plan), out_shape=jax.ShapeDtypeS...  41.1 us
    unnamed x1, local copies, waits for them, and re-layouts  1.88 us

profile of v2, /device:TPU:0, one launch (start us, length us, event | category | flops | bytes accessed | tf_op | source)
XLA Modules:
  0.0 43.0 jit_solution(9292834072837122602)
XLA Ops:
  0.0 41.1 %shard_map.55 = f32[4,4,16,512]{3,2,1,0:T(8,128)} custom-call(f32[4]{0:T(128)} %xy_hbm.1, f32[4]{0:T(128)} %z_hbm.1, f32[4,4,16,512]{3,2,1,0:T(8,128)} %fields.1, f32[2,4,16,512]{3,2,1,0:T(8,128)} %velocity.1, f32[4,16,512]{2,1,0:T(8,128)} %face_rate.1), custom_call_target="tpu_custom_call" | custom-call | flops 52428800 | bytes 2097152 | tf_op jit(solution)/shard_map/pallas_call | solution.py:541
  41.1 1.9 %copy.7 = f32[4,4,16,512]{3,2,1,0:T(8,128)} copy(f32[4,4,16,512]{3,2,1,0:T(8,128)} %shard_map.55) | data formatting | bytes 1048576

commit v3 on v2

--- a/solution.py
+++ b/solution.py
@@ -124,6 +124,9 @@
             device_id_type=MESH,
         )
 
+    def await_bytes(ref, semaphore):
+        pltpu.make_async_copy(ref, ref, semaphore).wait()
+
     def field_in(f):
         return pltpu.make_async_copy(
             fields.at[f], present.at[0, f, :, pl.ds(0, rows)], field_sem.at[f]
@@ -160,15 +163,15 @@
             remote(
                 source.at[..., pl.ds(0, halo), :],
                 target.at[..., pl.ds(rows, halo), :],
-                send_sem.at[0],
-                recv_sem.at[0],
+                send_sem,
+                recv_sem,
                 {"gy": lower_y},
             ),
             remote(
                 source.at[..., pl.ds(rows - halo, halo), :],
                 target.at[..., pl.ds(rows + halo, halo), :],
-                send_sem.at[1],
-                recv_sem.at[1],
+                send_sem,
+                recv_sem,
                 {"gy": upper_y},
             ),
         ]
@@ -176,15 +179,15 @@
     def halos(step, f):
         source = fields.at[f] if step == 0 else present.at[step, f]
         return halo_pair(
-            source, present.at[step, f], halo_send.at[step, f], halo_recv.at[step, f]
+            source, present.at[step, f], halo_send.at[step], halo_recv.at[step, f]
         )
 
     def rate_copy(offset):
         return remote(
             face_rate.at[:, :, lanes(plane_peer(offset))],
             rates_plane.at[mine1],
-            rate_send.at[offset - 1],
-            rate_recv.at[offset - 1],
+            rate_send.at[0],
+            rate_recv.at[0],
             plane_id(plane_peer(offset)),
         )
 
@@ -192,8 +195,8 @@
         return remote(
             send1.at[step, plane_peer(offset), f],
             recv1.at[step, mine1, f],
-            s1_send.at[step, f, offset - 1],
-            s1_recv.at[step, f, offset - 1],
+            s1_send.at[step],
+            s1_recv.at[step, f],
             plane_id(plane_peer(offset)),
         )
 
@@ -201,8 +204,8 @@
         return remote(
             back1.at[step, plane_peer(offset), f],
             home1.at[step, mine1, f],
-            b1_send.at[step, f, offset - 1],
-            b1_recv.at[step, f, offset - 1],
+            b1_send.at[step],
+            b1_recv.at[step, f],
             plane_id(plane_peer(offset)),
         )
 
@@ -216,7 +219,7 @@
             send2.at[step, f, part],
             recv2.at[step, inner, mine2],
             s2_send.at[step, f, part],
-            s2_recv.at[step, inner, mine2],
+            s2_recv.at[step, inner],
             stack_id(owner),
         )
 
@@ -227,12 +230,9 @@
             send_el.at[f, part],
             recv_el.at[inner, mine2],
             el_send.at[f, part],
-            el_recv.at[inner, mine2],
+            el_recv.at[inner],
             stack_id(owner),
         )
-
-    def arrival2(buffer, source_of, recv_sem, inner, source):
-        return remote(source_of, buffer.at[inner, source], recv_sem, recv_sem, stack_id(source))
 
     my_first = lax.div(mine2, per_field) * fields_each
     my_part = lax.rem(mine2, per_field)
@@ -243,18 +243,9 @@
         return remote(
             back2.at[step, inner, peer],
             home2.at[step, f, my_part],
-            b2_send.at[step, inner, offset - 1],
+            b2_send.at[step, inner],
             b2_recv.at[step, f, my_part],
             stack_id(peer),
-        )
-
-    def home_arrival(step, f, part):
-        return remote(
-            home2.at[step, f, part],
-            home2.at[step, f, part],
-            b2_recv.at[step, f, part],
-            b2_recv.at[step, f, part],
-            stack_id(owner_of(f, part)),
         )
 
     def as_owner(body):
@@ -273,7 +264,7 @@
     def rows_of(part):
         return slice(part * rows_each, (part + 1) * rows_each)
 
-    speed_halos = halo_pair(velocity, speed, speed_send, speed_recv)
+    speed_halos = halo_pair(velocity, speed, speed_send.at[0], speed_recv.at[0])
     for copy in speed_halos:
         copy.start()
 
@@ -307,8 +298,7 @@
 
     for copy in locals_in[3:]:
         copy.wait()
-    for copy in speed_halos:
-        copy.wait_recv()
+    await_bytes(speed.at[:, :, pl.ds(rows, 2 * halo)], speed_recv.at[0])
     for n in range(2):
         for k in range(layers):
             speed[n, k, : rows + halo] = 0.5 * ring(speed[n, k])
@@ -338,11 +328,7 @@
 
     def stack_factors():
         for inner in range(fields_each):
-            for offset in range(1, g2):
-                source = stack_peer(offset)
-                arrival2(
-                    recv_el, send_el.at[0, 0], el_recv.at[inner, source], inner, source
-                ).wait_recv()
+            await_bytes(recv_el.at[inner, pl.ds(0, g2 - 1)], el_recv.at[inner])
             total = tuple(recv_el[inner, 0, n] for n in range(3))
             for g in range(1, g2):
                 total, factors = join(total, tuple(recv_el[inner, g, n] for n in range(3)))
@@ -353,8 +339,7 @@
     def own_forward(step, f):
         if step == 0:
             field_in(f).wait()
-        for copy in halos(step, f):
-            copy.wait_recv()
+        await_bytes(present.at[step, f, :, pl.ds(rows, 2 * halo)], halo_recv.at[step, f])
         spread = xy_rate[f]
         centre = 1.0 - 4.0 * spread
         low = None
@@ -394,8 +379,7 @@
         recv1[step, mine1, f] = send1[step, mine1, f]
 
     def plane_forward(step, f):
-        for offset in range(1, g1):
-            out1(step, f, offset).wait_recv()
+        await_bytes(recv1.at[step, pl.ds(0, g1 - 1), f], s1_recv.at[step, f])
         low = recv1[step, 0, f, 0]
         high = recv1[step, 0, f, 1]
         for i in range(1, g1):
@@ -415,15 +399,7 @@
 
     def stack_solve(step):
         for inner in range(fields_each):
-            for offset in range(1, g2):
-                source = stack_peer(offset)
-                arrival2(
-                    recv2.at[step],
-                    send2.at[step, 0, 0],
-                    s2_recv.at[step, inner, source],
-                    inner,
-                    source,
-                ).wait_recv()
+            await_bytes(recv2.at[step, inner, pl.ds(0, g2 - 1)], s2_recv.at[step, inner])
             high = recv2[step, inner, 0, 1]
             meetings = []
             for g in range(1, g2):
@@ -444,7 +420,9 @@
             home2[step, my_first + inner, my_part] = back2[step, inner, mine2]
 
     def plane_backward(step, f):
-        parts(f, None, lambda part: home_arrival(step, f, part).wait_recv())
+        parts(
+            f, None, lambda part: await_bytes(home2.at[step, f, part], b2_recv.at[step, f, part])
+        )
         for part in range(per_field):
             cut = rows_of(part)
             base = home2[step, f, part, 0]
@@ -464,8 +442,7 @@
         home1[step, mine1, f] = back1[step, mine1, f]
 
     def own_backward(step, f):
-        for offset in range(1, g1):
-            in1(step, f, offset).wait_recv()
+        await_bytes(home1.at[step, pl.ds(0, g1 - 1), f], b1_recv.at[step, f])
         for c in range(g1):
             cut = slice(c * TILE_LANES, (c + 1) * TILE_LANES)
             base = home1[step, c, f, 0]
@@ -485,41 +462,47 @@
             for copy in halos(step + 1, f):
                 copy.start()
 
+    def sent_out(step):
+        await_bytes(present.at[step, :, :, pl.ds(rows, 2 * halo)], halo_send.at[step])
+        await_bytes(send1.at[step, pl.ds(0, g1 - 1)], s1_send.at[step])
+        each_field(lambda f: parts(f, None, lambda part: out2(step, f, part).wait_send()))
+
+    def sent_home(step):
+        def stack():
+            for inner in range(fields_each):
+                await_bytes(back2.at[step, inner, pl.ds(0, g2 - 1)], b2_send.at[step, inner])
+
+        as_owner(stack)
+        await_bytes(back1.at[step, pl.ds(0, g1 - 1)], b1_send.at[step])
+
+    each_field(functools.partial(own_forward, 0))
+    await_bytes(rates_plane.at[pl.ds(0, g1 - 1)], rate_recv.at[0])
+    each_field(plane_factors)
     for step in range(STEPS):
-        each_field(functools.partial(own_forward, step))
-        if step == 0:
-            for offset in range(1, g1):
-                rate_copy(offset).wait_recv()
-            each_field(plane_factors)
         each_field(functools.partial(plane_forward, step))
         if step == 0:
             as_owner(stack_factors)
         as_owner(functools.partial(stack_solve, step))
         each_field(functools.partial(plane_backward, step))
-        each_field(functools.partial(own_backward, step))
-
-    for copy in speed_halos:
-        copy.wait_send()
-    for offset in range(1, g1):
-        rate_copy(offset).wait_send()
-    each_field(lambda f: parts(f, None, lambda part: el_out(f, part).wait_send()))
-    for step in range(STEPS):
-
-        def sent(f, step=step):
-            for copy in halos(step, f):
-                copy.wait_send()
-            for offset in range(1, g1):
-                out1(step, f, offset).wait_send()
-                in1(step, f, offset).wait_send()
-            parts(f, None, lambda part: out2(step, f, part).wait_send())
-
-        def sent_back(step=step):
-            for inner in range(fields_each):
-                for offset in range(1, g2):
-                    in2(step, inner, offset).wait_send()
-
-        each_field(sent)
-        as_owner(sent_back)
+        if step == 0:
+            await_bytes(speed.at[:, :, pl.ds(rows, 2 * halo)], speed_send.at[0])
+            await_bytes(rates_plane.at[pl.ds(0, g1 - 1)], rate_send.at[0])
+            each_field(lambda f: parts(f, None, lambda part: el_out(f, part).wait_send()))
+        sent_out(step)
+        if step < STEPS - 1:
+            own_backward(step, 0)
+
+            def turn(f, carry, step=step):
+                own_backward(step, f)
+                own_forward(step + 1, f - 1)
+                return carry
+
+            lax.fori_loop(1, field_total, turn, 0)
+            own_forward(step + 1, field_total - 1)
+            sent_home(step)
+        else:
+            each_field(functools.partial(own_backward, step))
+            sent_home(step)
 
 
 def on_device(fields, velocity, face_rate, xy_rate, z_scale):
@@ -567,22 +550,22 @@
             vmem(fields_each, g2, 3, *share2),
             dma(5),
             dma(field_total),
-            dma(STEPS, field_total, 2),
-            dma(STEPS, field_total, 2),
-            dma(2),
-            dma(2),
-            dma(g1 - 1),
-            dma(g1 - 1),
-            dma(STEPS, field_total, g1 - 1),
-            dma(STEPS, field_total, g1 - 1),
-            dma(STEPS, field_total, g1 - 1),
-            dma(STEPS, field_total, g1 - 1),
+            dma(STEPS),
+            dma(STEPS, field_total),
+            dma(1),
+            dma(1),
+            dma(1),
+            dma(1),
+            dma(STEPS),
+            dma(STEPS, field_total),
+            dma(STEPS),
+            dma(STEPS, field_total),
             dma(STEPS, field_total, per_field),
-            dma(STEPS, fields_each, g2),
-            dma(STEPS, fields_each, g2 - 1),
+            dma(STEPS, fields_each),
+            dma(STEPS, fields_each),
             dma(STEPS, field_total, per_field),
             dma(field_total, per_field),
-            dma(fields_each, g2),
+            dma(fields_each),
         ],
         compiler_params=pltpu.CompilerParams(
             collective_id=0, has_side_effects=True, vmem_limit_bytes=60 * 1024 * 1024

time: 43.2 us -> 41 us (0.949)
  Pallas kernels: 41.1 us -> 39 us
    pallas_call x1, Pallas kernels: 41.1 us -> 39 us  [on_device(): pl.pallas_call(functools.partial(kernel, plan), out_shape=jax.ShapeDtypeS...]
where the time goes in v3:
time: 41 us; the launch traced here: 40.8 us
  Pallas kernels  39 us (95%)
  local copies, waits for them, and re-layouts  1.88 us (5%)
    pallas_call x1, Pallas kernels, on_device(): pl.pallas_call(functools.partial(kernel, plan), out_shape=jax.ShapeDtypeS...  39 us
    unnamed x1, local copies, waits for them, and re-layouts  1.88 us

profile of v3, /device:TPU:0, one launch (start us, length us, event | category | flops | bytes accessed | tf_op | source)
XLA Modules:
  0.0 40.8 jit_solution(1238229551773454927)
XLA Ops:
  0.0 39.0 %shard_map.55 = f32[4,4,16,512]{3,2,1,0:T(8,128)} custom-call(f32[4]{0:T(128)} %xy_hbm.1, f32[4]{0:T(128)} %z_hbm.1, f32[4,4,16,512]{3,2,1,0:T(8,128)} %fields.1, f32[2,4,16,512]{3,2,1,0:T(8,128)} %velocity.1, f32[4,16,512]{2,1,0:T(8,128)} %face_rate.1), custom_call_target="tpu_custom_call" | custom-call | flops 52428800 | bytes 2097152 | tf_op jit(solution)/shard_map/pallas_call | solution.py:524
  39.0 1.9 %copy.7 = f32[4,4,16,512]{3,2,1,0:T(8,128)} copy(f32[4,4,16,512]{3,2,1,0:T(8,128)} %shard_map.55) | data formatting | bytes 1048576

commit v4 on v3

--- a/solution.py
+++ b/solution.py
@@ -53,14 +53,13 @@
     coef1,
     held1,
     coef2,
+    held2,
     send1,
     recv1,
     back1,
     home1,
     send2,
     recv2,
-    back2,
-    home2,
     send_el,
     recv_el,
     local_sem,
@@ -77,12 +76,10 @@
     b1_recv,
     s2_send,
     s2_recv,
-    b2_send,
-    b2_recv,
     el_send,
     el_recv,
 ):
-    g1, g2, owners, per_field, fields_each, rows_each, gy_count = plan
+    g1, g2, rounds, gy_count = plan
     field_total, layers, rows, width = fields.shape
     halo = TILE_ROWS
     me = lax.axis_index("gz")
@@ -95,8 +92,14 @@
     def plane_peer(offset):
         return lax.rem(mine1 + offset, g1)
 
-    def stack_peer(offset):
-        return lax.rem(mine2 + offset, g2)
+    def stack_bit(t):
+        return lax.rem(lax.div(mine2, 2**t), 2)
+
+    def stack_peer(t):
+        return mine2 + (1 - 2 * stack_bit(t)) * 2**t
+
+    def pick(t, lower, upper):
+        return jnp.where(jnp.broadcast_to(stack_bit(t), lower.shape) == 0, lower, upper)
 
     def plane_id(position):
         return {"gz": mine2 * g1 + position}
@@ -152,11 +155,11 @@
         pl.semaphore_signal(
             barrier, inc=1, device_id=plane_id(plane_peer(offset)), device_id_type=MESH
         )
-    for offset in range(1, g2):
+    for t in range(rounds):
         pl.semaphore_signal(
-            barrier, inc=1, device_id=stack_id(stack_peer(offset)), device_id_type=MESH
-        )
-    pl.semaphore_wait(barrier, 2 + g1 - 1 + g2 - 1)
+            barrier, inc=1, device_id=stack_id(stack_peer(t)), device_id_type=MESH
+        )
+    pl.semaphore_wait(barrier, 2 + g1 - 1 + rounds)
 
     def halo_pair(source, target, send_sem, recv_sem):
         return [
@@ -209,60 +212,31 @@
             plane_id(plane_peer(offset)),
         )
 
-    def owner_of(f, part):
-        return lax.div(f, fields_each) * per_field + part
-
-    def out2(step, f, part):
-        owner = owner_of(f, part)
-        inner = lax.rem(f, fields_each)
+    last = rounds - 1
+
+    def payload2(buffer, step, t, f):
+        return buffer.at[step, t, f, pl.ds(0, 1 if t == last else 2)]
+
+    def payload_el(buffer, t, f):
+        return buffer.at[t, f, pl.ds(0, 1 if t == last else 3)]
+
+    def pair2(step, t, f):
         return remote(
-            send2.at[step, f, part],
-            recv2.at[step, inner, mine2],
-            s2_send.at[step, f, part],
-            s2_recv.at[step, inner],
-            stack_id(owner),
-        )
-
-    def el_out(f, part):
-        owner = owner_of(f, part)
-        inner = lax.rem(f, fields_each)
+            payload2(send2, step, t, f),
+            payload2(recv2, step, t, f),
+            s2_send.at[step, t],
+            s2_recv.at[step, t, f],
+            stack_id(stack_peer(t)),
+        )
+
+    def pair_el(t, f):
         return remote(
-            send_el.at[f, part],
-            recv_el.at[inner, mine2],
-            el_send.at[f, part],
-            el_recv.at[inner],
-            stack_id(owner),
-        )
-
-    my_first = lax.div(mine2, per_field) * fields_each
-    my_part = lax.rem(mine2, per_field)
-
-    def in2(step, inner, offset):
-        f = my_first + inner
-        peer = stack_peer(offset)
-        return remote(
-            back2.at[step, inner, peer],
-            home2.at[step, f, my_part],
-            b2_send.at[step, inner],
-            b2_recv.at[step, f, my_part],
-            stack_id(peer),
-        )
-
-    def as_owner(body):
-        if owners == g2:
-            body()
-        else:
-            pl.when(mine2 < owners)(body)
-
-    def parts(f, same, other):
-        for part in range(per_field):
-            own = owner_of(f, part) == mine2
-            if same is not None:
-                pl.when(own)(functools.partial(same, part))
-            pl.when(jnp.logical_not(own))(functools.partial(other, part))
-
-    def rows_of(part):
-        return slice(part * rows_each, (part + 1) * rows_each)
+            payload_el(send_el, t, f),
+            payload_el(recv_el, t, f),
+            el_send.at[t],
+            el_recv.at[t, f],
+            stack_id(stack_peer(t)),
+        )
 
     speed_halos = halo_pair(velocity, speed, speed_send.at[0], speed_recv.at[0])
     for copy in speed_halos:
@@ -316,25 +290,34 @@
                 total, factors = join(total, element)
                 for n in range(3):
                     coef1[n, i - 1, f] = factors[n]
-        inner = lax.rem(f, fields_each)
-        for part in range(per_field):
+        offer_element(0, f, total)
+
+    def offer_element(t, f, element):
+        if t < last:
             for n in range(3):
-                send_el[f, part, n] = total[n][rows_of(part)]
-
-        def same(part):
-            recv_el[inner, mine2] = send_el[f, part]
-
-        parts(f, same, lambda part: el_out(f, part).start())
-
-    def stack_factors():
-        for inner in range(fields_each):
-            await_bytes(recv_el.at[inner, pl.ds(0, g2 - 1)], el_recv.at[inner])
-            total = tuple(recv_el[inner, 0, n] for n in range(3))
-            for g in range(1, g2):
-                total, factors = join(total, tuple(recv_el[inner, g, n] for n in range(3)))
-                coef2[inner, 0, g - 1] = factors[1]
-                coef2[inner, 1, g - 1] = factors[2]
-            coef2[inner, 0, g2 - 1] = 1.0 / (total[0] + total[2])
+                send_el[t, f, n] = element[n]
+        else:
+            closing = element[0] + element[2]
+            inverse = 1.0 / closing
+            ratio = element[0] * inverse
+            coef2[0, t, f] = ratio
+            coef2[1, t, f] = inverse
+            send_el[t, f, 0] = pick(t, closing, element[1] + ratio * element[2])
+        pair_el(t, f).start()
+
+    def stack_factors(t, f):
+        await_bytes(payload_el(recv_el, t, f), el_recv.at[t, f])
+        if t < last:
+            mine = tuple(send_el[t, f, n] for n in range(3))
+            other = tuple(recv_el[t, f, n] for n in range(3))
+            lower = tuple(pick(t, a, b) for a, b in zip(mine, other))
+            upper = tuple(pick(t, b, a) for a, b in zip(mine, other))
+            total, factors = join(lower, upper)
+            for n in range(3):
+                coef2[n, t, f] = factors[n]
+            offer_element(t + 1, f, total)
+        else:
+            coef2[2, t, f] = 1.0 / (send_el[t, f, 0] + recv_el[t, f, 0])
 
     def own_forward(step, f):
         if step == 0:
@@ -387,56 +370,50 @@
             held1[i - 1, f] = meeting
             low = low + coef1[0, i - 1, f] * meeting
             high = recv1[step, i, f, 1] + coef1[1, i - 1, f] * meeting
-        for part in range(per_field):
-            send2[step, f, part, 0] = low[rows_of(part)]
-            send2[step, f, part, 1] = high[rows_of(part)]
-        inner = lax.rem(f, fields_each)
-
-        def same(part):
-            recv2[step, inner, mine2] = send2[step, f, part]
-
-        parts(f, same, lambda part: out2(step, f, part).start())
-
-    def stack_solve(step):
-        for inner in range(fields_each):
-            await_bytes(recv2.at[step, inner, pl.ds(0, g2 - 1)], s2_recv.at[step, inner])
-            high = recv2[step, inner, 0, 1]
-            meetings = []
-            for g in range(1, g2):
-                meeting = high + recv2[step, inner, g, 0]
-                meetings.append(meeting)
-                high = recv2[step, inner, g, 1] + coef2[inner, 0, g - 1] * meeting
-            value = high * coef2[inner, 0, g2 - 1]
-            back2[step, inner, g2 - 1, 1] = value
-            for g in range(g2 - 1, 0, -1):
-                value = (
-                    meetings[g - 1] * coef2[inner, 1, g - 1] + coef2[inner, 0, g - 1] * value
-                )
-                back2[step, inner, g, 0] = value
-                back2[step, inner, g - 1, 1] = value
-            back2[step, inner, 0, 0] = jnp.zeros_like(value)
-            for offset in range(1, g2):
-                in2(step, inner, offset).start()
-            home2[step, my_first + inner, my_part] = back2[step, inner, mine2]
-
-    def plane_backward(step, f):
-        parts(
-            f, None, lambda part: await_bytes(home2.at[step, f, part], b2_recv.at[step, f, part])
-        )
-        for part in range(per_field):
-            cut = rows_of(part)
-            base = home2[step, f, part, 0]
-            value = home2[step, f, part, 1]
-            back1[step, g1 - 1, f, 1, cut] = value
-            for i in range(g1 - 1, 0, -1):
-                value = (
-                    held1[i - 1, f, cut] * coef1[2, i - 1, f, cut]
-                    + coef1[0, i - 1, f, cut] * base
-                    + coef1[1, i - 1, f, cut] * value
-                )
-                back1[step, i, f, 0, cut] = value
-                back1[step, i - 1, f, 1, cut] = value
-            back1[step, 0, f, 0, cut] = base
+        offer(step, 0, f, low, high)
+
+    def offer(step, t, f, low, high):
+        if t < last:
+            send2[step, t, f, 0] = low
+        else:
+            send2[step, t, f, 0] = pick(t, high, low + coef2[0, t, f] * high)
+        send2[step, t, f, 1] = high
+        pair2(step, t, f).start()
+
+    def stack_round(step, t, f):
+        await_bytes(payload2(recv2, step, t, f), s2_recv.at[step, t, f])
+        low = send2[step, t, f, 0]
+        high = send2[step, t, f, 1]
+        other_low = recv2[step, t, f, 0]
+        if t < last:
+            other_high = recv2[step, t, f, 1]
+            meeting = pick(t, high, other_high) + pick(t, other_low, low)
+            held2[t, f] = meeting
+            low, high = (
+                pick(t, low, other_low) + coef2[0, t, f] * meeting,
+                pick(t, other_high, high) + coef2[1, t, f] * meeting,
+            )
+            offer(step, t + 1, f, low, high)
+            return
+        middle = (low + other_low) * coef2[2, t, f]
+        top = high * coef2[1, t, f] + coef2[0, t, f] * middle
+        base = pick(t, jnp.zeros_like(middle), middle)
+        value = pick(t, middle, top)
+        for r in range(last - 1, -1, -1):
+            middle = (
+                held2[r, f] * coef2[2, r, f] + coef2[0, r, f] * base + coef2[1, r, f] * value
+            )
+            base, value = pick(r, base, middle), pick(r, middle, value)
+        back1[step, g1 - 1, f, 1] = value
+        for i in range(g1 - 1, 0, -1):
+            value = (
+                held1[i - 1, f] * coef1[2, i - 1, f]
+                + coef1[0, i - 1, f] * base
+                + coef1[1, i - 1, f] * value
+            )
+            back1[step, i, f, 0] = value
+            back1[step, i - 1, f, 1] = value
+        back1[step, 0, f, 0] = base
         for offset in range(1, g1):
             in1(step, f, offset).start()
         home1[step, mine1, f] = back1[step, mine1, f]
@@ -465,14 +442,10 @@
     def sent_out(step):
         await_bytes(present.at[step, :, :, pl.ds(rows, 2 * halo)], halo_send.at[step])
         await_bytes(send1.at[step, pl.ds(0, g1 - 1)], s1_send.at[step])
-        each_field(lambda f: parts(f, None, lambda part: out2(step, f, part).wait_send()))
+        for t in range(rounds):
+            await_bytes(send2.at[step, t, :, pl.ds(0, 1 if t == last else 2)], s2_send.at[step, t])
 
     def sent_home(step):
-        def stack():
-            for inner in range(fields_each):
-                await_bytes(back2.at[step, inner, pl.ds(0, g2 - 1)], b2_send.at[step, inner])
-
-        as_owner(stack)
         await_bytes(back1.at[step, pl.ds(0, g1 - 1)], b1_send.at[step])
 
     each_field(functools.partial(own_forward, 0))
@@ -480,14 +453,15 @@
     each_field(plane_factors)
     for step in range(STEPS):
         each_field(functools.partial(plane_forward, step))
-        if step == 0:
-            as_owner(stack_factors)
-        as_owner(functools.partial(stack_solve, step))
-        each_field(functools.partial(plane_backward, step))
+        for t in range(rounds):
+            if step == 0:
+                each_field(functools.partial(stack_factors, t))
+            each_field(functools.partial(stack_round, step, t))
         if step == 0:
             await_bytes(speed.at[:, :, pl.ds(rows, 2 * halo)], speed_send.at[0])
             await_bytes(rates_plane.at[pl.ds(0, g1 - 1)], rate_send.at[0])
-            each_field(lambda f: parts(f, None, lambda part: el_out(f, part).wait_send()))
+            for t in range(rounds):
+                await_bytes(send_el.at[t, :, pl.ds(0, 1 if t == last else 3)], el_send.at[t])
         sent_out(step)
         if step < STEPS - 1:
             own_backward(step, 0)
@@ -511,14 +485,11 @@
     field_total, layers, rows, width = fields.shape
     g1 = width // TILE_LANES
     g2 = gz_count // g1
-    owners = min(g2, field_total * rows // TILE_ROWS)
-    per_field = max(1, owners // field_total)
-    fields_each = max(1, field_total // owners)
-    rows_each = rows // per_field
-    plan = (g1, g2, owners, per_field, fields_each, rows_each, gy_count)
+    rounds = g2.bit_length() - 1
+    assert g1 * 2**rounds == gz_count
+    plan = (g1, g2, rounds, gy_count)
     extent = rows + 2 * TILE_ROWS
     share1 = (rows, TILE_LANES)
-    share2 = (rows_each, TILE_LANES)
     vmem = lambda *shape: pltpu.VMEM(shape, jnp.float32)
     dma = lambda *shape: pltpu.SemaphoreType.DMA(shape)
     return pl.pallas_call(
@@ -537,17 +508,16 @@
             vmem(layers - 1, field_total, rows, width),
             vmem(3, g1 - 1, field_total, *share1),
             vmem(g1 - 1, field_total, *share1),
-            vmem(fields_each, 2, g2, *share2),
+            vmem(3, rounds, field_total, *share1),
+            vmem(rounds, field_total, *share1),
             vmem(STEPS, g1, field_total, 2, *share1),
             vmem(STEPS, g1, field_total, 2, *share1),
             vmem(STEPS, g1, field_total, 2, *share1),
             vmem(STEPS, g1, field_total, 2, *share1),
-            vmem(STEPS, field_total, per_field, 2, *share2),
-            vmem(STEPS, fields_each, g2, 2, *share2),
-            vmem(STEPS, fields_each, g2, 2, *share2),
-            vmem(STEPS, field_total, per_field, 2, *share2),
-            vmem(field_total, per_field, 3, *share2),
-            vmem(fields_each, g2, 3, *share2),
+            vmem(STEPS, rounds, field_total, 2, *share1),
+            vmem(STEPS, rounds, field_total, 2, *share1),
+            vmem(rounds, field_total, 3, *share1),
+            vmem(rounds, field_total, 3, *share1),
             dma(5),
             dma(field_total),
             dma(STEPS),
@@ -560,12 +530,10 @@
             dma(STEPS, field_total),
             dma(STEPS),
             dma(STEPS, field_total),
-            dma(STEPS, field_total, per_field),
-            dma(STEPS, fields_each),
-            dma(STEPS, fields_each),
-            dma(STEPS, field_total, per_field),
-            dma(field_total, per_field),
-            dma(fields_each),
+            dma(STEPS, rounds),
+            dma(STEPS, rounds, field_total),
+            dma(rounds),
+            dma(rounds, field_total),
         ],
         compiler_params=pltpu.CompilerParams(
             collective_id=0, has_side_effects=True, vmem_limit_bytes=60 * 1024 * 1024

time: 41 us -> 39.2 us (0.956)
  Pallas kernels: 39 us -> 37.2 us
    pallas_call x1, Pallas kernels: 39 us -> 37.2 us  [on_device(): pl.pallas_call(functools.partial(kernel, plan), out_shape=jax.ShapeDtypeS...]
where the time goes in v4:
time: 39.2 us; the launch traced here: 39.1 us
  Pallas kernels  37.2 us (95%)
  local copies, waits for them, and re-layouts  1.88 us (5%)
    pallas_call x1, Pallas kernels, on_device(): pl.pallas_call(functools.partial(kernel, plan), out_shape=jax.ShapeDtypeS...  37.2 us
    unnamed x1, local copies, waits for them, and re-layouts  1.88 us

profile of v4, /device:TPU:0, one launch (start us, length us, event | category | flops | bytes accessed | tf_op | source)
XLA Modules:
  0.0 39.1 jit_solution(14895285319832033243)
XLA Ops:
  0.0 37.2 %shard_map.55 = f32[4,4,16,512]{3,2,1,0:T(8,128)} custom-call(f32[4]{0:T(128)} %xy_hbm.1, f32[4]{0:T(128)} %z_hbm.1, f32[4,4,16,512]{3,2,1,0:T(8,128)} %fields.1, f32[2,4,16,512]{3,2,1,0:T(8,128)} %velocity.1, f32[4,16,512]{2,1,0:T(8,128)} %face_rate.1), custom_call_target="tpu_custom_call" | custom-call | flops 52428800 | bytes 2097152 | tf_op jit(solution)/shard_map/pallas_call | solution.py:495
  37.2 1.9 %copy.7 = f32[4,4,16,512]{3,2,1,0:T(8,128)} copy(f32[4,4,16,512]{3,2,1,0:T(8,128)} %shard_map.55) | data formatting | bytes 1048576

commit v5 on v4

--- a/solution.py
+++ b/solution.py
@@ -270,8 +270,7 @@
         )
         return jnp.concatenate([block[:rows], edge], axis=0)
 
-    for copy in locals_in[3:]:
-        copy.wait()
+    locals_in[3].wait()
     await_bytes(speed.at[:, :, pl.ds(rows, 2 * halo)], speed_recv.at[0])
     for n in range(2):
         for k in range(layers):
@@ -343,9 +342,9 @@
             north = pltpu.roll(sectioned, extent - 1, 0)[:rows]
             south = pltpu.roll(sectioned, 1, 0)[:rows]
             inner_weights = tuple(w[:rows] for w in weights[:4]) + (centre,)
-            explicit = 0.5 * (
-                q[:rows] + stencil(sectioned[:rows], north, south, inner_weights)
-            )
+            explicit = q[:rows] + stencil(sectioned[:rows], north, south, inner_weights)
+            if step < STEPS - 1:
+                explicit = 0.5 * explicit
             if k == 0:
                 high = explicit
             else:
@@ -448,14 +447,25 @@
     def sent_home(step):
         await_bytes(back1.at[step, pl.ds(0, g1 - 1)], b1_send.at[step])
 
-    each_field(functools.partial(own_forward, 0))
-    await_bytes(rates_plane.at[pl.ds(0, g1 - 1)], rate_recv.at[0])
-    each_field(plane_factors)
+    def opening(f):
+        own_forward(0, f)
+
+        @pl.when(f == 0)
+        def plane():
+            locals_in[4].wait()
+            await_bytes(rates_plane.at[pl.ds(0, g1 - 1)], rate_recv.at[0])
+            each_field(plane_factors)
+
+        for t in range(rounds):
+
+            @pl.when(f == min(t + 2, field_total - 1))
+            def stack(t=t):
+                each_field(functools.partial(stack_factors, t))
+
+    each_field(opening)
     for step in range(STEPS):
         each_field(functools.partial(plane_forward, step))
         for t in range(rounds):
-            if step == 0:
-                each_field(functools.partial(stack_factors, t))
             each_field(functools.partial(stack_round, step, t))
         if step == 0:
             await_bytes(speed.at[:, :, pl.ds(rows, 2 * halo)], speed_send.at[0])
@@ -492,7 +502,7 @@
     share1 = (rows, TILE_LANES)
     vmem = lambda *shape: pltpu.VMEM(shape, jnp.float32)
     dma = lambda *shape: pltpu.SemaphoreType.DMA(shape)
-    return pl.pallas_call(
+    doubled = pl.pallas_call(
         functools.partial(kernel, plan),
         out_shape=jax.ShapeDtypeStruct(fields.shape, jnp.float32),
         in_specs=[pl.BlockSpec(memory_space=pl.ANY)] * 5,
@@ -542,6 +552,7 @@
             flops=400 * fields.size, bytes_accessed=16 * fields.size, transcendentals=0
         ),
     )(xy_rate, z_scale, fields, velocity, face_rate)
+    return 0.5 * doubled
 
 
 def solution(mesh):

time: 39.2 us -> 45 us (1.15)
  Pallas kernels: 37.2 us -> 42.9 us
  other arithmetic: 0 us -> 1.88 us
  local copies, waits for them, and re-layouts: 1.88 us -> 0 us
    pallas_call x1, Pallas kernels: 37.2 us -> 42.9 us  [on_device(): pl.pallas_call(functools.partial(kernel, plan), out_shape=jax.ShapeDtypeS...]
    unnamed x1 -> x0, local copies, waits for them, and re-layouts: 1.88 us -> none
    mul x0 -> x1, other arithmetic: none -> 1.88 us  [on_device(): return 0.5 * doubled]
where the time goes in v5:
time: 45 us; the launch traced here: 44.8 us
  Pallas kernels  42.9 us (95%)
  other arithmetic  1.88 us (4%)
    pallas_call x1, Pallas kernels, on_device(): pl.pallas_call(functools.partial(kernel, plan), out_shape=jax.ShapeDtypeS...  42.9 us
    mul x1, other arithmetic, on_device(): return 0.5 * doubled  1.88 us

profile of v5, /device:TPU:0, one launch (start us, length us, event | category | flops | bytes accessed | tf_op | source)
XLA Modules:
  0.0 44.8 jit_solution(4878945504613730380)
XLA Ops:
  0.0 42.9 %shard_map.55 = f32[4,4,16,512]{3,2,1,0:T(8,128)} custom-call(f32[4]{0:T(128)} %xy_hbm.1, f32[4]{0:T(128)} %z_hbm.1, f32[4,4,16,512]{3,2,1,0:T(8,128)} %fields.1, f32[2,4,16,512]{3,2,1,0:T(8,128)} %velocity.1, f32[4,16,512]{2,1,0:T(8,128)} %face_rate.1), custom_call_target="tpu_custom_call" | custom-call | flops 52428800 | bytes 2097152 | tf_op jit(solution)/shard_map/pallas_call | solution.py:505
  42.9 1.9 %broadcast_multiply_fusion = f32[4,4,16,512]{3,2,1,0:T(8,128)} fusion(f32[4,4,16,512]{3,2,1,0:T(8,128)} %shard_map.55), kind=kLoop, calls=%fused_computation | loop fusion | flops 131072 | bytes 1048576 | tf_op jit(solution)/shard_map/mul | solution.py:555

commit v6 on v4

--- a/solution.py
+++ b/solution.py
@@ -21,9 +21,15 @@
     return (east * eastern + west * western) + (up * north + down * south) + centre * q
 
 
+def reciprocal(value):
+    estimate = pl.reciprocal(value, approx=True)
+    estimate = estimate * (2.0 - value * estimate)
+    return estimate * (2.0 - value * estimate)
+
+
 def join(lower, upper):
     between = lower[2] + upper[1]
-    inverse = 1.0 / (lower[0] + upper[0] + between)
+    inverse = reciprocal(lower[0] + upper[0] + between)
     to_low = lower[0] * inverse
     to_high = upper[0] * inverse
     element = (to_low * upper[0], lower[1] + to_low * between, upper[2] + to_high * between)
@@ -54,6 +60,7 @@
     held1,
     coef2,
     held2,
+    result,
     send1,
     recv1,
     back1,
@@ -64,6 +71,7 @@
     recv_el,
     local_sem,
     field_sem,
+    out_sem,
     halo_send,
     halo_recv,
     speed_send,
@@ -135,6 +143,9 @@
             fields.at[f], present.at[0, f, :, pl.ds(0, rows)], field_sem.at[f]
         )
 
+    def field_out(f):
+        return pltpu.make_async_copy(result.at[f], out.at[f], out_sem.at[f])
+
     locals_in = [
         pltpu.make_async_copy(z_hbm, z_scale, local_sem.at[0]),
         pltpu.make_async_copy(xy_hbm, xy_rate, local_sem.at[1]),
@@ -277,20 +288,26 @@
         for k in range(layers):
             speed[n, k, : rows + halo] = 0.5 * ring(speed[n, k])
 
-    def plane_factors(f):
-        scale = z_scale[f]
-        total = None
-        for i in range(g1):
-            element = layer_element(scale * rates_plane[i, 0])
-            for k in range(1, layers):
-                element, ignored = join(element, layer_element(scale * rates_plane[i, k]))
-            if total is None:
-                total = element
-            else:
-                total, factors = join(total, element)
-                for n in range(3):
-                    coef1[n, i - 1, f] = factors[n]
-        offer_element(0, f, total)
+    def plane_factors():
+        totals = []
+        for f in range(field_total):
+            scale = z_scale[f]
+            total = None
+            for i in range(g1):
+                element = layer_element(scale * rates_plane[i, 0])
+                for k in range(1, layers):
+                    element, ignored = join(element, layer_element(scale * rates_plane[i, k]))
+                if total is None:
+                    total = element
+                else:
+                    total, factors = join(total, element)
+                    for n in range(3):
+                        coef1[n, i - 1, f] = factors[n]
+            totals.append(total)
+        for f in range(field_total):
+            offer_element(0, f, totals[f])
+        for f in range(field_total):
+            pair_el(0, f).start()
 
     def offer_element(t, f, element):
         if t < last:
@@ -298,15 +315,22 @@
                 send_el[t, f, n] = element[n]
         else:
             closing = element[0] + element[2]
-            inverse = 1.0 / closing
+            inverse = reciprocal(closing)
             ratio = element[0] * inverse
             coef2[0, t, f] = ratio
             coef2[1, t, f] = inverse
             send_el[t, f, 0] = pick(t, closing, element[1] + ratio * element[2])
-        pair_el(t, f).start()
-
-    def stack_factors(t, f):
-        await_bytes(payload_el(recv_el, t, f), el_recv.at[t, f])
+
+    def stack_factors(t):
+        for f in range(field_total):
+            await_bytes(payload_el(recv_el, t, f), el_recv.at[t, f])
+        for f in range(field_total):
+            stack_factors_of(t, f)
+        if t < last:
+            for f in range(field_total):
+                pair_el(t + 1, f).start()
+
+    def stack_factors_of(t, f):
         if t < last:
             mine = tuple(send_el[t, f, n] for n in range(3))
             other = tuple(recv_el[t, f, n] for n in range(3))
@@ -317,7 +341,7 @@
                 coef2[n, t, f] = factors[n]
             offer_element(t + 1, f, total)
         else:
-            coef2[2, t, f] = 1.0 / (send_el[t, f, 0] + recv_el[t, f, 0])
+            coef2[2, t, f] = reciprocal(send_el[t, f, 0] + recv_el[t, f, 0])
 
     def own_forward(step, f):
         if step == 0:
@@ -432,12 +456,14 @@
                         + coef0[1, k, f, :, cut] * value
                     )
                 if step == STEPS - 1:
-                    out[f, k, :, cut] = value
+                    result[f, k, :, cut] = value
                 else:
                     present[step + 1, f, k, :rows, cut] = value
         if step < STEPS - 1:
             for copy in halos(step + 1, f):
                 copy.start()
+        else:
+            field_out(f).start()
 
     def sent_out(step):
         await_bytes(present.at[step, :, :, pl.ds(rows, 2 * halo)], halo_send.at[step])
@@ -450,12 +476,12 @@
 
     each_field(functools.partial(own_forward, 0))
     await_bytes(rates_plane.at[pl.ds(0, g1 - 1)], rate_recv.at[0])
-    each_field(plane_factors)
+    plane_factors()
     for step in range(STEPS):
         each_field(functools.partial(plane_forward, step))
         for t in range(rounds):
             if step == 0:
-                each_field(functools.partial(stack_factors, t))
+                stack_factors(t)
             each_field(functools.partial(stack_round, step, t))
         if step == 0:
             await_bytes(speed.at[:, :, pl.ds(rows, 2 * halo)], speed_send.at[0])
@@ -477,6 +503,7 @@
         else:
             each_field(functools.partial(own_backward, step))
             sent_home(step)
+            each_field(lambda f: field_out(f).wait())
 
 
 def on_device(fields, velocity, face_rate, xy_rate, z_scale):
@@ -496,7 +523,7 @@
         functools.partial(kernel, plan),
         out_shape=jax.ShapeDtypeStruct(fields.shape, jnp.float32),
         in_specs=[pl.BlockSpec(memory_space=pl.ANY)] * 5,
-        out_specs=pl.BlockSpec(memory_space=pltpu.VMEM),
+        out_specs=pl.BlockSpec(memory_space=pl.ANY),
         scratch_shapes=[
             pltpu.SMEM((field_total,), jnp.float32),
             pltpu.SMEM((field_total,), jnp.float32),
@@ -510,6 +537,7 @@
             vmem(g1 - 1, field_total, *share1),
             vmem(3, rounds, field_total, *share1),
             vmem(rounds, field_total, *share1),
+            vmem(field_total, layers, rows, width),
             vmem(STEPS, g1, field_total, 2, *share1),
             vmem(STEPS, g1, field_total, 2, *share1),
             vmem(STEPS, g1, field_total, 2, *share1),
@@ -519,6 +547,7 @@
             vmem(rounds, field_total, 3, *share1),
             vmem(rounds, field_total, 3, *share1),
             dma(5),
+            dma(field_total),
             dma(field_total),
             dma(STEPS),
             dma(STEPS, field_total),

time: 39.2 us -> 40 us (1.020)
  Pallas kernels: 37.2 us -> 37.9 us
    pallas_call x1, Pallas kernels: 37.2 us -> 37.9 us  [on_device(): pl.pallas_call(functools.partial(kernel, plan), out_shape=jax.ShapeDtypeS...]
where the time goes in v6:
time: 40 us; the launch traced here: 39.8 us
  Pallas kernels  37.9 us (95%)
  local copies, waits for them, and re-layouts  1.88 us (5%)
    pallas_call x1, Pallas kernels, on_device(): pl.pallas_call(functools.partial(kernel, plan), out_shape=jax.ShapeDtypeS...  37.9 us
    unnamed x1, local copies, waits for them, and re-layouts  1.88 us

profile of v6, /device:TPU:0, one launch (start us, length us, event | category | flops | bytes accessed | tf_op | source)
XLA Modules:
  0.0 39.8 jit_solution(16052852622610991013)
XLA Ops:
  0.0 37.9 %shard_map.55 = f32[4,4,16,512]{3,2,1,0:T(8,128)} custom-call(f32[4]{0:T(128)} %xy_hbm.1, f32[4]{0:T(128)} %z_hbm.1, f32[4,4,16,512]{3,2,1,0:T(8,128)} %fields.1, f32[2,4,16,512]{3,2,1,0:T(8,128)} %velocity.1, f32[4,16,512]{2,1,0:T(8,128)} %face_rate.1), custom_call_target="tpu_custom_call" | custom-call | flops 52428800 | bytes 2097152 | tf_op jit(solution)/shard_map/pallas_call | solution.py:522
  37.9 1.9 %copy.7 = f32[4,4,16,512]{3,2,1,0:T(8,128)} copy(f32[4,4,16,512]{3,2,1,0:T(8,128)} %shard_map.55) | data formatting | bytes 1048576

commit v7 on v6

--- a/solution.py
+++ b/solution.py
@@ -10,6 +10,7 @@
 STEPS = 2
 TILE_ROWS = 8
 TILE_LANES = 128
+EDGE = 2
 MESH = pl.DeviceIdType.MESH
 
 
@@ -146,6 +147,9 @@
     def field_out(f):
         return pltpu.make_async_copy(result.at[f], out.at[f], out_sem.at[f])
 
+    for ref in (present, speed):
+        ref[..., rows:, :] = jnp.zeros(ref.shape[:-2] + (halo, width), jnp.float32)
+
     locals_in = [
         pltpu.make_async_copy(z_hbm, z_scale, local_sem.at[0]),
         pltpu.make_async_copy(xy_hbm, xy_rate, local_sem.at[1]),
@@ -175,15 +179,15 @@
     def halo_pair(source, target, send_sem, recv_sem):
         return [
             remote(
-                source.at[..., pl.ds(0, halo), :],
-                target.at[..., pl.ds(rows, halo), :],
+                source.at[..., pl.ds(0, EDGE), :],
+                target.at[..., pl.ds(rows, EDGE), :],
                 send_sem,
                 recv_sem,
                 {"gy": lower_y},
             ),
             remote(
-                source.at[..., pl.ds(rows - halo, halo), :],
-                target.at[..., pl.ds(rows + halo, halo), :],
+                source.at[..., pl.ds(rows - EDGE, EDGE), :],
+                target.at[..., pl.ds(rows + halo - EDGE, EDGE), :],
                 send_sem,
                 recv_sem,
                 {"gy": upper_y},
@@ -274,19 +278,12 @@
 
     each_field(own_factors)
 
-    def ring(block):
-        place = lax.broadcasted_iota(jnp.int32, (halo, width), 0)
-        edge = jnp.where(
-            place < halo // 2, block[rows : rows + halo], block[rows + halo : rows + 2 * halo]
-        )
-        return jnp.concatenate([block[:rows], edge], axis=0)
-
     for copy in locals_in[3:]:
         copy.wait()
-    await_bytes(speed.at[:, :, pl.ds(rows, 2 * halo)], speed_recv.at[0])
+    await_bytes(speed.at[:, :, pl.ds(0, 2 * EDGE)], speed_recv.at[0])
     for n in range(2):
         for k in range(layers):
-            speed[n, k, : rows + halo] = 0.5 * ring(speed[n, k])
+            speed[n, k] = 0.5 * speed[n, k]
 
     def plane_factors():
         totals = []
@@ -346,16 +343,16 @@
     def own_forward(step, f):
         if step == 0:
             field_in(f).wait()
-        await_bytes(present.at[step, f, :, pl.ds(rows, 2 * halo)], halo_recv.at[step, f])
+        await_bytes(present.at[step, f, :, pl.ds(0, 2 * EDGE)], halo_recv.at[step, f])
         spread = xy_rate[f]
         centre = 1.0 - 4.0 * spread
         low = None
         high = None
         extent = rows + halo
         for k in range(layers):
-            q = ring(present[step, f, k])
-            along_x = speed[0, k, :extent]
-            along_y = speed[1, k, :extent]
+            q = present[step, f, k]
+            along_x = speed[0, k]
+            along_y = speed[1, k]
             weights = (
                 spread - along_x,
                 spread + along_x,
@@ -466,7 +463,7 @@
             field_out(f).start()
 
     def sent_out(step):
-        await_bytes(present.at[step, :, :, pl.ds(rows, 2 * halo)], halo_send.at[step])
+        await_bytes(present.at[step, :, :, pl.ds(0, 2 * EDGE)], halo_send.at[step])
         await_bytes(send1.at[step, pl.ds(0, g1 - 1)], s1_send.at[step])
         for t in range(rounds):
             await_bytes(send2.at[step, t, :, pl.ds(0, 1 if t == last else 2)], s2_send.at[step, t])
@@ -484,7 +481,7 @@
                 stack_factors(t)
             each_field(functools.partial(stack_round, step, t))
         if step == 0:
-            await_bytes(speed.at[:, :, pl.ds(rows, 2 * halo)], speed_send.at[0])
+            await_bytes(speed.at[:, :, pl.ds(0, 2 * EDGE)], speed_send.at[0])
             await_bytes(rates_plane.at[pl.ds(0, g1 - 1)], rate_send.at[0])
             for t in range(rounds):
                 await_bytes(send_el.at[t, :, pl.ds(0, 1 if t == last else 3)], el_send.at[t])
@@ -515,7 +512,7 @@
     rounds = g2.bit_length() - 1
     assert g1 * 2**rounds == gz_count
     plan = (g1, g2, rounds, gy_count)
-    extent = rows + 2 * TILE_ROWS
+    extent = rows + TILE_ROWS
     share1 = (rows, TILE_LANES)
     vmem = lambda *shape: pltpu.VMEM(shape, jnp.float32)
     dma = lambda *shape: pltpu.SemaphoreType.DMA(shape)

time: 40 us -> 38.6 us (0.965)
  Pallas kernels: 37.9 us -> 36.6 us
    pallas_call x1, Pallas kernels: 37.9 us -> 36.6 us  [on_device(): pl.pallas_call(functools.partial(kernel, plan), out_shape=jax.ShapeDtypeS...]
where the time goes in v7:
time: 38.6 us; the launch traced here: 38.5 us
  Pallas kernels  36.6 us (95%)
  local copies, waits for them, and re-layouts  1.88 us (5%)
    pallas_call x1, Pallas kernels, on_device(): pl.pallas_call(functools.partial(kernel, plan), out_shape=jax.ShapeDtypeS...  36.6 us
    unnamed x1, local copies, waits for them, and re-layouts  1.88 us

profile of v7, /device:TPU:0, one launch (start us, length us, event | category | flops | bytes accessed | tf_op | source)
XLA Modules:
  0.0 38.5 jit_solution(17791451633351918029)
XLA Ops:
  0.0 36.6 %shard_map.55 = f32[4,4,16,512]{3,2,1,0:T(8,128)} custom-call(f32[4]{0:T(128)} %xy_hbm.1, f32[4]{0:T(128)} %z_hbm.1, f32[4,4,16,512]{3,2,1,0:T(8,128)} %fields.1, f32[2,4,16,512]{3,2,1,0:T(8,128)} %velocity.1, f32[4,16,512]{2,1,0:T(8,128)} %face_rate.1), custom_call_target="tpu_custom_call" | custom-call | flops 52428800 | bytes 2097152 | tf_op jit(solution)/shard_map/pallas_call | solution.py:519
  36.6 1.9 %copy.7 = f32[4,4,16,512]{3,2,1,0:T(8,128)} copy(f32[4,4,16,512]{3,2,1,0:T(8,128)} %shard_map.55) | data formatting | bytes 1048576

commit v8 on v7

--- a/solution.py
+++ b/solution.py
@@ -88,7 +88,7 @@
     el_send,
     el_recv,
 ):
-    g1, g2, rounds, gy_count = plan
+    g1, g2, rounds, gy_count, chunk = plan
     field_total, layers, rows, width = fields.shape
     halo = TILE_ROWS
     me = lax.axis_index("gz")
@@ -125,6 +125,16 @@
             return carry
 
         lax.fori_loop(0, field_total, step_body, 0)
+
+    def each_chunk(body):
+        def step_body(c, carry):
+            body(c)
+            return carry
+
+        lax.fori_loop(0, field_total // chunk, step_body, 0)
+
+    def of_chunk(c):
+        return pl.ds(c * chunk, chunk)
 
     def remote(source, target, send_sem, recv_sem, device):
         return pltpu.make_async_remote_copy(
@@ -209,38 +219,38 @@
             plane_id(plane_peer(offset)),
         )
 
-    def out1(step, f, offset):
+    def out1(step, c, offset):
         return remote(
-            send1.at[step, plane_peer(offset), f],
-            recv1.at[step, mine1, f],
+            send1.at[step, plane_peer(offset), of_chunk(c)],
+            recv1.at[step, mine1, of_chunk(c)],
             s1_send.at[step],
-            s1_recv.at[step, f],
+            s1_recv.at[step, c],
             plane_id(plane_peer(offset)),
         )
 
-    def in1(step, f, offset):
+    def in1(step, c, offset):
         return remote(
-            back1.at[step, plane_peer(offset), f],
-            home1.at[step, mine1, f],
+            back1.at[step, plane_peer(offset), of_chunk(c)],
+            home1.at[step, mine1, of_chunk(c)],
             b1_send.at[step],
-            b1_recv.at[step, f],
+            b1_recv.at[step, c],
             plane_id(plane_peer(offset)),
         )
 
     last = rounds - 1
 
-    def payload2(buffer, step, t, f):
-        return buffer.at[step, t, f, pl.ds(0, 1 if t == last else 2)]
+    def payload2(buffer, step, t, c):
+        return buffer.at[step, t, c, pl.ds(0, 1 if t == last else 2)]
 
     def payload_el(buffer, t, f):
         return buffer.at[t, f, pl.ds(0, 1 if t == last else 3)]
 
-    def pair2(step, t, f):
+    def pair2(step, t, c):
         return remote(
-            payload2(send2, step, t, f),
-            payload2(recv2, step, t, f),
+            payload2(send2, step, t, c),
+            payload2(recv2, step, t, c),
             s2_send.at[step, t],
-            s2_recv.at[step, t, f],
+            s2_recv.at[step, t, c],
             stack_id(stack_peer(t)),
         )
 
@@ -378,69 +388,79 @@
             cut = slice(c * TILE_LANES, (c + 1) * TILE_LANES)
             send1[step, c, f, 0] = low[:, cut]
             send1[step, c, f, 1] = high[:, cut]
-        for offset in range(1, g1):
-            out1(step, f, offset).start()
         recv1[step, mine1, f] = send1[step, mine1, f]
 
-    def plane_forward(step, f):
-        await_bytes(recv1.at[step, pl.ds(0, g1 - 1), f], s1_recv.at[step, f])
-        low = recv1[step, 0, f, 0]
-        high = recv1[step, 0, f, 1]
+        @pl.when(lax.rem(f, chunk) == chunk - 1)
+        def send():
+            for offset in range(1, g1):
+                out1(step, lax.div(f, chunk), offset).start()
+
+    def plane_forward(step, c):
+        fs = of_chunk(c)
+        await_bytes(recv1.at[step, pl.ds(0, g1 - 1), fs], s1_recv.at[step, c])
+        low = recv1[step, 0, fs, 0]
+        high = recv1[step, 0, fs, 1]
         for i in range(1, g1):
-            meeting = high + recv1[step, i, f, 0]
-            held1[i - 1, f] = meeting
-            low = low + coef1[0, i - 1, f] * meeting
-            high = recv1[step, i, f, 1] + coef1[1, i - 1, f] * meeting
-        offer(step, 0, f, low, high)
-
-    def offer(step, t, f, low, high):
+            meeting = high + recv1[step, i, fs, 0]
+            held1[i - 1, fs] = meeting
+            low = low + coef1[0, i - 1, fs] * meeting
+            high = recv1[step, i, fs, 1] + coef1[1, i - 1, fs] * meeting
+        offer(step, 0, c, low, high)
+
+    def offer(step, t, c, low, high):
+        fs = of_chunk(c)
         if t < last:
-            send2[step, t, f, 0] = low
+            send2[step, t, c, 0] = low
         else:
-            send2[step, t, f, 0] = pick(t, high, low + coef2[0, t, f] * high)
-        send2[step, t, f, 1] = high
-        pair2(step, t, f).start()
-
-    def stack_round(step, t, f):
-        await_bytes(payload2(recv2, step, t, f), s2_recv.at[step, t, f])
-        low = send2[step, t, f, 0]
-        high = send2[step, t, f, 1]
-        other_low = recv2[step, t, f, 0]
+            send2[step, t, c, 0] = pick(t, high, low + coef2[0, t, fs] * high)
+        send2[step, t, c, 1] = high
+        pair2(step, t, c).start()
+
+    def stack_round(step, t, c):
+        fs = of_chunk(c)
+        await_bytes(payload2(recv2, step, t, c), s2_recv.at[step, t, c])
+        low = send2[step, t, c, 0]
+        high = send2[step, t, c, 1]
+        other_low = recv2[step, t, c, 0]
         if t < last:
-            other_high = recv2[step, t, f, 1]
+            other_high = recv2[step, t, c, 1]
             meeting = pick(t, high, other_high) + pick(t, other_low, low)
-            held2[t, f] = meeting
+            held2[t, fs] = meeting
             low, high = (
-                pick(t, low, other_low) + coef2[0, t, f] * meeting,
-                pick(t, other_high, high) + coef2[1, t, f] * meeting,
+                pick(t, low, other_low) + coef2[0, t, fs] * meeting,
+                pick(t, other_high, high) + coef2[1, t, fs] * meeting,
             )
-            offer(step, t + 1, f, low, high)
+            offer(step, t + 1, c, low, high)
             return
-        middle = (low + other_low) * coef2[2, t, f]
-        top = high * coef2[1, t, f] + coef2[0, t, f] * middle
+        middle = (low + other_low) * coef2[2, t, fs]
+        top = high * coef2[1, t, fs] + coef2[0, t, fs] * middle
         base = pick(t, jnp.zeros_like(middle), middle)
         value = pick(t, middle, top)
         for r in range(last - 1, -1, -1):
             middle = (
-                held2[r, f] * coef2[2, r, f] + coef2[0, r, f] * base + coef2[1, r, f] * value
+                held2[r, fs] * coef2[2, r, fs] + coef2[0, r, fs] * base + coef2[1, r, fs] * value
             )
             base, value = pick(r, base, middle), pick(r, middle, value)
-        back1[step, g1 - 1, f, 1] = value
+        back1[step, g1 - 1, fs, 1] = value
         for i in range(g1 - 1, 0, -1):
             value = (
-                held1[i - 1, f] * coef1[2, i - 1, f]
-                + coef1[0, i - 1, f] * base
-                + coef1[1, i - 1, f] * value
+                held1[i - 1, fs] * coef1[2, i - 1, fs]
+                + coef1[0, i - 1, fs] * base
+                + coef1[1, i - 1, fs] * value
             )
-            back1[step, i, f, 0] = value
-            back1[step, i - 1, f, 1] = value
-        back1[step, 0, f, 0] = base
+            back1[step, i, fs, 0] = value
+            back1[step, i - 1, fs, 1] = value
+        back1[step, 0, fs, 0] = base
         for offset in range(1, g1):
-            in1(step, f, offset).start()
-        home1[step, mine1, f] = back1[step, mine1, f]
+            in1(step, c, offset).start()
+        home1[step, mine1, fs] = back1[step, mine1, fs]
 
     def own_backward(step, f):
-        await_bytes(home1.at[step, pl.ds(0, g1 - 1), f], b1_recv.at[step, f])
+        @pl.when(lax.rem(f, chunk) == 0)
+        def arrive():
+            c = lax.div(f, chunk)
+            await_bytes(home1.at[step, pl.ds(0, g1 - 1), of_chunk(c)], b1_recv.at[step, c])
+
         for c in range(g1):
             cut = slice(c * TILE_LANES, (c + 1) * TILE_LANES)
             base = home1[step, c, f, 0]
@@ -475,11 +495,11 @@
     await_bytes(rates_plane.at[pl.ds(0, g1 - 1)], rate_recv.at[0])
     plane_factors()
     for step in range(STEPS):
-        each_field(functools.partial(plane_forward, step))
+        each_chunk(functools.partial(plane_forward, step))
         for t in range(rounds):
             if step == 0:
                 stack_factors(t)
-            each_field(functools.partial(stack_round, step, t))
+            each_chunk(functools.partial(stack_round, step, t))
         if step == 0:
             await_bytes(speed.at[:, :, pl.ds(0, 2 * EDGE)], speed_send.at[0])
             await_bytes(rates_plane.at[pl.ds(0, g1 - 1)], rate_send.at[0])
@@ -487,7 +507,7 @@
                 await_bytes(send_el.at[t, :, pl.ds(0, 1 if t == last else 3)], el_send.at[t])
         sent_out(step)
         if step < STEPS - 1:
-            own_backward(step, 0)
+            own_backward(step, jnp.int32(0))
 
             def turn(f, carry, step=step):
                 own_backward(step, f)
@@ -495,7 +515,7 @@
                 return carry
 
             lax.fori_loop(1, field_total, turn, 0)
-            own_forward(step + 1, field_total - 1)
+            own_forward(step + 1, jnp.int32(field_total - 1))
             sent_home(step)
         else:
             each_field(functools.partial(own_backward, step))
@@ -511,7 +531,8 @@
     g2 = gz_count // g1
     rounds = g2.bit_length() - 1
     assert g1 * 2**rounds == gz_count
-    plan = (g1, g2, rounds, gy_count)
+    chunk = 2 if field_total % 2 == 0 else 1
+    plan = (g1, g2, rounds, gy_count, chunk)
     extent = rows + TILE_ROWS
     share1 = (rows, TILE_LANES)
     vmem = lambda *shape: pltpu.VMEM(shape, jnp.float32)
@@ -539,8 +560,8 @@
             vmem(STEPS, g1, field_total, 2, *share1),
             vmem(STEPS, g1, field_total, 2, *share1),
             vmem(STEPS, g1, field_total, 2, *share1),
-            vmem(STEPS, rounds, field_total, 2, *share1),
-            vmem(STEPS, rounds, field_total, 2, *share1),
+            vmem(STEPS, rounds, field_total // chunk, 2, chunk, *share1),
+            vmem(STEPS, rounds, field_total // chunk, 2, chunk, *share1),
             vmem(rounds, field_total, 3, *share1),
             vmem(rounds, field_total, 3, *share1),
             dma(5),
@@ -553,11 +574,11 @@
             dma(1),
             dma(1),
             dma(STEPS),
-            dma(STEPS, field_total),
+            dma(STEPS, field_total // chunk),
             dma(STEPS),
-            dma(STEPS, field_total),
+            dma(STEPS, field_total // chunk),
             dma(STEPS, rounds),
-            dma(STEPS, rounds, field_total),
+            dma(STEPS, rounds, field_total // chunk),
             dma(rounds),
             dma(rounds, field_total),
         ],

time: 38.6 us -> 40.1 us (1.039)
  Pallas kernels: 36.6 us -> 38.1 us
    pallas_call x1, Pallas kernels: 36.6 us -> 38.1 us  [on_device(): pl.pallas_call(functools.partial(kernel, plan), out_shape=jax.ShapeDtypeS...]
where the time goes in v8:
time: 40.1 us; the launch traced here: 40 us
  Pallas kernels  38.1 us (95%)
  local copies, waits for them, and re-layouts  1.88 us (5%)
    pallas_call x1, Pallas kernels, on_device(): pl.pallas_call(functools.partial(kernel, plan), out_shape=jax.ShapeDtypeS...  38.1 us
    unnamed x1, local copies, waits for them, and re-layouts  1.88 us

profile of v8, /device:TPU:0, one launch (start us, length us, event | category | flops | bytes accessed | tf_op | source)
XLA Modules:
  0.0 40.0 jit_solution(557709558238818923)
XLA Ops:
  0.0 38.1 %shard_map.55 = f32[4,4,16,512]{3,2,1,0:T(8,128)} custom-call(f32[4]{0:T(128)} %xy_hbm.1, f32[4]{0:T(128)} %z_hbm.1, f32[4,4,16,512]{3,2,1,0:T(8,128)} %fields.1, f32[2,4,16,512]{3,2,1,0:T(8,128)} %velocity.1, f32[4,16,512]{2,1,0:T(8,128)} %face_rate.1), custom_call_target="tpu_custom_call" | custom-call | flops 52428800 | bytes 2097152 | tf_op jit(solution)/shard_map/pallas_call | solution.py:540
  38.1 1.9 %copy.7 = f32[4,4,16,512]{3,2,1,0:T(8,128)} copy(f32[4,4,16,512]{3,2,1,0:T(8,128)} %shard_map.55) | data formatting | bytes 1048576

commit v9 on v7

--- a/solution.py
+++ b/solution.py
@@ -475,7 +475,9 @@
     await_bytes(rates_plane.at[pl.ds(0, g1 - 1)], rate_recv.at[0])
     plane_factors()
     for step in range(STEPS):
-        each_field(functools.partial(plane_forward, step))
+        if step == 0:
+            plane_forward(step, 0)
+        lax.fori_loop(1, field_total, lambda f, carry: plane_forward(step, f) or carry, 0)
         for t in range(rounds):
             if step == 0:
                 stack_factors(t)
@@ -495,6 +497,7 @@
                 return carry
 
             lax.fori_loop(1, field_total, turn, 0)
+            plane_forward(step + 1, 0)
             own_forward(step + 1, field_total - 1)
             sent_home(step)
         else:

time: 38.6 us -> 40.3 us (1.044)
  Pallas kernels: 36.6 us -> 38.3 us
    pallas_call x1, Pallas kernels: 36.6 us -> 38.3 us  [on_device(): pl.pallas_call(functools.partial(kernel, plan), out_shape=jax.ShapeDtypeS...]
where the time goes in v9:
time: 40.3 us; the launch traced here: 40.2 us
  Pallas kernels  38.3 us (95%)
  local copies, waits for them, and re-layouts  1.88 us (5%)
    pallas_call x1, Pallas kernels, on_device(): pl.pallas_call(functools.partial(kernel, plan), out_shape=jax.ShapeDtypeS...  38.3 us
    unnamed x1, local copies, waits for them, and re-layouts  1.88 us

profile of v9, /device:TPU:0, one launch (start us, length us, event | category | flops | bytes accessed | tf_op | source)
XLA Modules:
  0.0 40.2 jit_solution(13185757339989267217)
XLA Ops:
  0.0 38.3 %shard_map.55 = f32[4,4,16,512]{3,2,1,0:T(8,128)} custom-call(f32[4]{0:T(128)} %xy_hbm.1, f32[4]{0:T(128)} %z_hbm.1, f32[4,4,16,512]{3,2,1,0:T(8,128)} %fields.1, f32[2,4,16,512]{3,2,1,0:T(8,128)} %velocity.1, f32[4,16,512]{2,1,0:T(8,128)} %face_rate.1), custom_call_target="tpu_custom_call" | custom-call | flops 52428800 | bytes 2097152 | tf_op jit(solution)/shard_map/pallas_call | solution.py:522
  38.3 1.9 %copy.7 = f32[4,4,16,512]{3,2,1,0:T(8,128)} copy(f32[4,4,16,512]{3,2,1,0:T(8,128)} %shard_map.55) | data formatting | bytes 1048576
